TPU v7x, 32 devices: a whole 2x2x4 slice. The times are simulated.
32 devices in a mesh: dp: 8 (over z, x), tensor: 4 (over y, core).
Axes of the slice: x: 2, y: 2, z: 4, core: 2. Of those that a mesh axis runs over, the one named last changes fastest.
Arguments:
- inputs: bfloat16 [8192, 1024], P(('dp', 'tensor')), may hold values from -6 to 6
- cotangent: bfloat16 [8192, 1024], P(('dp', 'tensor')), may hold values from -6 to 6
- gain_in: bfloat16 [1024], P('dp'), may hold values from 0.5 to 1.5
- query_weight: bfloat16 [1024, 512], P('dp', 'tensor'), may hold values from -0.1875 to 0.1875
- shared_matrix: bfloat16 [1024, 512], P('dp'), may hold values from -0.1875 to 0.1875
- attention_out: bfloat16 [1024, 512], P('dp', 'tensor'), may hold values from -2 to 2
- mixer_in: bfloat16 [1024, 2, 1536], P('dp', None, 'tensor'), may hold values from -0.1875 to 0.1875
- step_weight: bfloat16 [1024, 24], P('dp', 'tensor'), may hold values from -0.1875 to 0.1875
- filter_inner: bfloat16 [5, 1536], P(None, 'tensor'), may hold values from -3 to 3
- filter_state: bfloat16 [256, 5], P('dp'), may hold values from -3 to 3
- step_bias: bfloat16 [24], P('tensor'), may hold values from -4 to -1
- log_decay: bfloat16 [24], P('tensor'), may hold values from -7 to 2.796875
- skip_gain: bfloat16 [24], P('tensor'), may hold values from 0.5 to 1.5
- mixer_gain: bfloat16 [1536], P('tensor'), may hold values from 0.5 to 1.5
- mixer_out: bfloat16 [1024, 1536], P('dp', 'tensor'), may hold values from -0.15625 to 0.15625
- gain_post: bfloat16 [1024], P('dp'), may hold values from 0.5 to 1.5
- gate_up: bfloat16 [1024, 2, 2048], P('dp', None, 'tensor'), may hold values from -0.1875 to 0.1875
- down_weight: bfloat16 [1024, 2048], P('dp', 'tensor'), may hold values from -0.125 to 0.125
Outputs:
- output: bfloat16 [8192, 1024], P(('dp', 'tensor'))
- back_inputs: float32 [8192, 1024], P(('dp', 'tensor'))
- back_gain_in: float32 [1024], P('dp')
- back_query: float32 [1024, 512], P('dp', 'tensor')
- back_shared: float32 [1024, 512], P('dp')
- back_attention: float32 [1024, 512], P('dp', 'tensor')
- back_mixer_in: float32 [1024, 2, 1536], P('dp', None, 'tensor')
- back_step: float32 [1024, 24], P('dp', 'tensor')
- back_filter_inner: float32 [5, 1536], P(None, 'tensor')
- back_filter_state: float32 [256, 5], P('dp')
- back_step_bias: float32 [24], P('tensor')
- back_log_decay: float32 [24], P('tensor')
- back_skip_gain: float32 [24], P('tensor')
- back_mixer_gain: float32 [1536], P('tensor')
- back_mixer_out: float32 [1024, 1536], P('dp', 'tensor')
- back_gain_post: float32 [1024], P('dp')
- back_gate_up: float32 [1024, 2, 2048], P('dp', None, 'tensor')
- back_down: float32 [1024, 2048], P('dp', 'tensor')
All inputs are finite; a program needn't handle non-finite values.
Results may differ from a plain program's by a relative error of at most 0.03.
Values may be sent and summed in bfloat16 or wider, within the bound.
A program may use at most 192 MiB of HBM per device.

v0:
```python
import jax
import jax.numpy as jnp
from jax import lax
from jax.sharding import PartitionSpec as P

QUERY_HEADS = 8
HEAD_SIZE = 64
KEY_VALUE_HEADS = 2
NH = 24
PH = 64
BLK = 128
QB = 512


epsilon = 1e-05
rope_base = 100000000000.0
highest_precision = lax.Precision.HIGHEST


def as_sent(x):

    def short(part):
        return part.astype(jnp.bfloat16) if part.dtype == jnp.float32 else part

    return jax.tree.map(short, x)


def norm_scale(values):
    return lax.rsqrt(jnp.mean(values * values, axis=-1, keepdims=True) + epsilon)


def rotary_embed(values, sequence_length, sign):
    half = values.shape[-1] // 2
    position = jnp.arange(sequence_length, dtype=jnp.float32)
    frequency = rope_base ** (-jnp.arange(half, dtype=jnp.float32) * 2.0 / values.shape[-1])
    angle = position[:, None] * frequency[None, :]
    cosine = jnp.cos(angle)[:, None, :]
    sine = sign * jnp.sin(angle)[:, None, :]
    first = values[..., :half]
    second = values[..., half:]
    return jnp.concatenate(
        [first * cosine - second * sine, second * cosine + first * sine], axis=-1
    )


def causal_filter(values, taps, bias):
    width = taps.shape[0]
    sequence_length = values.shape[0]
    padded = jnp.pad(values, ((width - 1, 0), (0, 0)))
    total = bias[None, :] + jnp.zeros_like(values)
    for offset in range(width):
        total = total + taps[offset][None, :] * padded[offset : offset + sequence_length]
    return total


def mixer_input(inner_raw, state_raw, step_raw, filter_inner, filter_state, step_bias):
    kernel = filter_inner.shape[0] - 1
    inner = jax.nn.silu(causal_filter(inner_raw, filter_inner[:kernel], filter_inner[kernel]))
    state_in = jax.nn.silu(
        causal_filter(state_raw, jnp.transpose(filter_state[:, :kernel]), filter_state[:, kernel])
    )
    step_size = jax.nn.softplus(step_raw + step_bias[None, :])
    return (inner, state_in, step_size)


def state_scan(inner, state_in, step_size, gate_z, log_decay, skip_gain, block):
    sequence_length, channels = inner.shape
    heads = step_size.shape[1]
    head = channels // heads
    state_width = state_in.shape[1] // 2
    count = sequence_length // block
    inner_blocks = inner.reshape(count, block, heads, head)
    state_input_keys = state_in[:, :state_width].reshape(count, block, state_width)
    state_output_reads = state_in[:, state_width:].reshape(count, block, state_width)
    rate = step_size * (-jnp.exp(log_decay))[None, :]
    running = jnp.cumsum(rate.reshape(count, block, heads), axis=1)
    step_blocks = step_size.reshape(count, block, heads)
    within_group = jnp.einsum(
        "xfw,xkw->xfk", state_output_reads, state_input_keys, precision=highest_precision
    )
    lower = jnp.arange(block)[:, None] >= jnp.arange(block)[None, :]
    spread = running[:, :, None, :] - running[:, None, :, :]
    decay = jnp.exp(jnp.where(lower[None, :, :, None], spread, -1e30))
    mixing = within_group[..., None] * decay * step_blocks[:, None, :, :]
    local_out = jnp.einsum("clrh,crhp->clhp", mixing, inner_blocks, precision=highest_precision)
    tail = jnp.exp(running[:, -1:, :] - running) * step_blocks
    block_state = jnp.einsum(
        "crh,crhp,crn->chpn", tail, inner_blocks, state_input_keys, precision=highest_precision
    )
    total_decay = jnp.exp(running[:, -1, :])

    def advance(carry, pieces):
        fade, fresh = pieces
        return (carry * fade[:, None, None] + fresh, carry)

    zero_state = jnp.zeros((heads, head, state_width), inner.dtype)
    final, entering = lax.scan(advance, zero_state, (total_decay, block_state))
    carried = (
        jnp.einsum("cln,chpn->clhp", state_output_reads, entering, precision=highest_precision)
        * jnp.exp(running)[..., None]
    )
    result = (local_out + carried).reshape(sequence_length, channels) + inner * jnp.repeat(
        skip_gain, head
    )[None, :]
    return result * jax.nn.silu(gate_z)


def attend(query_low, keys_reduced, values_reduced, block):
    sequence_length, heads, head = query_low.shape
    scale = head ** (-0.5)
    count = sequence_length // block
    columns = jnp.arange(sequence_length)

    def one_block(index):
        start = index * block
        rows = lax.dynamic_slice_in_dim(query_low, start, block, 0)
        scores = (
            jnp.einsum("qhd,kd->hqk", rows, keys_reduced, preferred_element_type=jnp.float32)
            * scale
        )
        visible = (start + jnp.arange(block))[:, None] >= columns[None, :]
        scores = jnp.where(visible[None], scores, -1e30)
        peak = jnp.max(scores, axis=-1, keepdims=True)
        weights = jnp.exp(scores - peak)
        total = jnp.sum(weights, axis=-1, keepdims=True)
        shares_low = (weights / total).astype(jnp.bfloat16)
        mixed = jnp.einsum(
            "hqk,kd->qhd", shares_low, values_reduced, preferred_element_type=jnp.float32
        )
        return (mixed, (peak + jnp.log(total))[..., 0])

    mixed, log_total = lax.map(one_block, jnp.arange(count))
    return (mixed.reshape(sequence_length, heads * head), log_total)


def attend_back(query_low, keys_reduced, values_reduced, log_total, back_mixed_low, block):
    sequence_length, heads, head = query_low.shape
    scale = head ** (-0.5)
    count = sequence_length // block
    columns = jnp.arange(sequence_length)
    back_view = back_mixed_low.reshape(sequence_length, heads, head)

    def one_block(carry, pieces):
        back_keys, back_values = carry
        index, log_rows = pieces
        start = index * block
        rows = lax.dynamic_slice_in_dim(query_low, start, block, 0)
        back_rows = lax.dynamic_slice_in_dim(back_view, start, block, 0)
        scores = (
            jnp.einsum("qhd,kd->hqk", rows, keys_reduced, preferred_element_type=jnp.float32)
            * scale
        )
        visible = (start + jnp.arange(block))[:, None] >= columns[None, :]
        scores = jnp.where(visible[None], scores, -1e30)
        shares = jnp.where(visible[None], jnp.exp(scores - log_rows[..., None]), 0.0)
        back_shares = jnp.einsum(
            "qhd,kd->hqk", back_rows, values_reduced, preferred_element_type=jnp.float32
        )
        inner = jnp.sum(shares * back_shares, axis=-1, keepdims=True)
        back_scores = (shares * (back_shares - inner)).astype(jnp.bfloat16)
        back_query = (
            jnp.einsum("hqk,kd->qhd", back_scores, keys_reduced, preferred_element_type=jnp.float32)
            * scale
        )
        back_keys = (
            back_keys
            + jnp.einsum("hqk,qhd->kd", back_scores, rows, preferred_element_type=jnp.float32)
            * scale
        )
        back_values = back_values + jnp.einsum(
            "hqk,qhd->kd",
            shares.astype(jnp.bfloat16),
            back_rows,
            preferred_element_type=jnp.float32,
        )
        return ((back_keys, back_values), back_query)

    empty = jnp.zeros((sequence_length, head), jnp.float32)
    (back_keys, back_values), back_query = lax.scan(
        one_block, (empty, empty), (jnp.arange(count), log_total)
    )
    return (back_query.reshape(sequence_length, heads, head), back_keys, back_values)


def gather_rows(values):
    return lax.all_gather(values, "tensor", axis=0, tiled=True)


def scatter_rows(values):
    return lax.psum_scatter(values, "tensor", scatter_dimension=0, tiled=True).astype(jnp.float32)


def scatter_grads(values):
    return jax.tree.map(
        lambda part: part.astype(jnp.float32),
        lax.psum_scatter(as_sent(values), "tensor", scatter_dimension=0, tiled=True),
    )


def body(
    inputs,
    cotangent,
    gain_in,
    query_weight,
    shared_matrix,
    attention_out,
    mixer_in,
    step_weight,
    filter_inner,
    filter_state,
    step_bias,
    log_decay,
    skip_gain,
    mixer_gain,
    mixer_out,
    gain_post,
    gate_up,
    down_weight,
):
    tensor_position = lax.axis_index("tensor")
    (
        gain_in_all,
        query_all,
        shared_all,
        attention_all,
        mixer_in_all,
        step_all,
        filter_state_all,
        mixer_out_all,
        gain_post_all,
        gate_up_all,
        down_all,
    ) = (
        lax.all_gather(gain_in, "dp", axis=0, tiled=True),
        lax.all_gather(query_weight, "dp", axis=0, tiled=True),
        lax.all_gather(shared_matrix, "dp", axis=0, tiled=True),
        lax.all_gather(attention_out, "dp", axis=0, tiled=True),
        lax.all_gather(mixer_in, "dp", axis=0, tiled=True),
        lax.all_gather(step_weight, "dp", axis=0, tiled=True),
        lax.all_gather(filter_state, "dp", axis=0, tiled=True),
        lax.all_gather(mixer_out, "dp", axis=0, tiled=True),
        lax.all_gather(gain_post, "dp", axis=0, tiled=True),
        lax.all_gather(gate_up, "dp", axis=0, tiled=True),
        lax.all_gather(down_weight, "dp", axis=0, tiled=True),
    )
    local_heads = query_all.shape[1] // HEAD_SIZE
    head_group = tensor_position * local_heads // (QUERY_HEADS // KEY_VALUE_HEADS)
    key_value_width = KEY_VALUE_HEADS * HEAD_SIZE
    channels_all = NH * PH
    filter_inner_f = filter_inner.astype(jnp.float32)
    step_bias_f = step_bias.astype(jnp.float32)
    log_decay_f = log_decay.astype(jnp.float32)
    skip_gain_f = skip_gain.astype(jnp.float32)
    mixer_gain_f = mixer_gain.astype(jnp.float32)
    inputs_f = inputs.astype(jnp.float32)
    scale_in = norm_scale(inputs_f)
    normed_in = inputs_f * scale_in
    rows_in_low = (normed_in * gain_in_all.astype(jnp.float32)).astype(jnp.bfloat16)
    seq_in = gather_rows(rows_in_low)
    sequence_length = seq_in.shape[0]
    query = jnp.dot(seq_in, query_all, preferred_element_type=jnp.float32)
    query_low = rotary_embed(
        query.reshape(sequence_length, local_heads, HEAD_SIZE), sequence_length, 1.0
    ).astype(jnp.bfloat16)
    key_cols = lax.dynamic_slice_in_dim(shared_all, head_group * HEAD_SIZE, HEAD_SIZE, 1)
    value_cols = lax.dynamic_slice_in_dim(
        shared_all, key_value_width + head_group * HEAD_SIZE, HEAD_SIZE, 1
    )
    used_cols = jnp.concatenate(
        [key_cols, value_cols, shared_all[:, 2 * key_value_width :]], axis=1
    )
    shared_projection = jnp.dot(seq_in, used_cols, preferred_element_type=jnp.float32)
    keys_reduced = rotary_embed(shared_projection[:, None, :HEAD_SIZE], sequence_length, 1.0)[
        :, 0
    ].astype(jnp.bfloat16)
    values_reduced = shared_projection[:, HEAD_SIZE : 2 * HEAD_SIZE].astype(jnp.bfloat16)
    state_raw = shared_projection[:, 2 * HEAD_SIZE :]
    mixed, log_total = attend(query_low, keys_reduced, values_reduced, QB)
    mixed_low = mixed.astype(jnp.bfloat16)
    attention_part = jnp.dot(mixed_low, attention_all.T, preferred_element_type=jnp.float32)
    mixer_raw = jnp.einsum("sd,dcf->scf", seq_in, mixer_in_all, preferred_element_type=jnp.float32)
    gate_z = mixer_raw[:, 0]
    step_raw = jnp.dot(seq_in, step_all, preferred_element_type=jnp.float32)
    (inner, state_in, step_size), mixer_back = jax.vjp(
        mixer_input,
        mixer_raw[:, 1],
        state_raw,
        step_raw,
        filter_inner_f,
        filter_state_all.astype(jnp.float32),
        step_bias_f,
    )
    inner_low = inner.astype(jnp.bfloat16)
    state_low = state_in.astype(jnp.bfloat16)

    def scan_piece(inner_v, state_v, step_v, gate_v, decay_v, skip_v):
        return state_scan(inner_v, state_v, step_v, gate_v, decay_v, skip_v, BLK)

    gated, scan_back = jax.vjp(
        scan_piece,
        inner_low.astype(jnp.float32),
        state_low.astype(jnp.float32),
        step_size,
        gate_z,
        log_decay_f,
        skip_gain_f,
    )
    total_squares = lax.psum(jnp.sum(gated * gated, axis=1), "tensor")
    gated_scale = lax.rsqrt(total_squares / channels_all + epsilon)[:, None]
    gated_norm = gated * gated_scale
    mixer_low = (gated_norm * mixer_gain_f).astype(jnp.bfloat16)
    mixer_part = jnp.dot(mixer_low, mixer_out_all.T, preferred_element_type=jnp.float32)
    branch_low = (attention_part + mixer_part).astype(jnp.bfloat16)
    hidden = inputs_f + scatter_rows(branch_low)
    scale_post = norm_scale(hidden)
    normed_post = hidden * scale_post
    rows_post_low = (normed_post * gain_post_all.astype(jnp.float32)).astype(jnp.bfloat16)
    seq_post = gather_rows(rows_post_low)
    gate_values = jnp.einsum(
        "sd,dcf->scf", seq_post, gate_up_all, preferred_element_type=jnp.float32
    )
    gate = gate_values[:, 0]
    upper = gate_values[:, 1]
    activated_low = (jax.nn.silu(gate) * upper).astype(jnp.bfloat16)
    down_low = jnp.dot(activated_low, down_all.T, preferred_element_type=jnp.float32).astype(
        jnp.bfloat16
    )
    output = (hidden + scatter_rows(down_low)).astype(jnp.bfloat16)
    (
        gain_in_all,
        query_all,
        shared_all,
        attention_all,
        mixer_in_all,
        step_all,
        filter_state_all,
        mixer_out_all,
        gain_post_all,
        gate_up_all,
        down_all,
    ) = (
        lax.all_gather(gain_in, "dp", axis=0, tiled=True),
        lax.all_gather(query_weight, "dp", axis=0, tiled=True),
        lax.all_gather(shared_matrix, "dp", axis=0, tiled=True),
        lax.all_gather(attention_out, "dp", axis=0, tiled=True),
        lax.all_gather(mixer_in, "dp", axis=0, tiled=True),
        lax.all_gather(step_weight, "dp", axis=0, tiled=True),
        lax.all_gather(filter_state, "dp", axis=0, tiled=True),
        lax.all_gather(mixer_out, "dp", axis=0, tiled=True),
        lax.all_gather(gain_post, "dp", axis=0, tiled=True),
        lax.all_gather(gate_up, "dp", axis=0, tiled=True),
        lax.all_gather(down_weight, "dp", axis=0, tiled=True),
    )
    back_seq = gather_rows(cotangent)
    back_act = jnp.dot(back_seq, down_all, preferred_element_type=jnp.float32)
    sigmoid_gate = jax.nn.sigmoid(gate)
    back_gate = back_act * upper * sigmoid_gate * (1.0 + gate * (1.0 - sigmoid_gate))
    back_upper = back_act * jax.nn.silu(gate)
    back_gu_low = jnp.stack([back_gate, back_upper], axis=1).astype(jnp.bfloat16)
    back_down_w = jnp.dot(back_seq.T, activated_low, preferred_element_type=jnp.float32)
    back_gate_up_w = jnp.einsum(
        "sd,scf->dcf", seq_post, back_gu_low, preferred_element_type=jnp.float32
    )
    back_post_part = jnp.einsum(
        "scf,dcf->sd", back_gu_low, gate_up_all, preferred_element_type=jnp.float32
    )
    back_post = scatter_grads(back_post_part)
    back_gain_post = jnp.sum(back_post * normed_post, axis=0)
    back_norm_post = back_post * gain_post_all.astype(jnp.float32)
    back_hidden = cotangent.astype(jnp.float32) + scale_post * (
        back_norm_post - normed_post * jnp.mean(back_norm_post * normed_post, axis=1, keepdims=True)
    )
    back_mix = gather_rows(back_hidden.astype(jnp.bfloat16))
    back_norm = jnp.dot(back_mix, mixer_out_all, preferred_element_type=jnp.float32)
    back_mixer_out_w = jnp.dot(back_mix.T, mixer_low, preferred_element_type=jnp.float32)
    back_mixer_gain = jnp.sum(back_norm * gated_norm, axis=0)
    back_scaled = back_norm * mixer_gain_f
    inner_total = lax.psum(jnp.sum(back_scaled * gated_norm, axis=1), "tensor")
    back_gated = gated_scale * (back_scaled - gated_norm * (inner_total / channels_all)[:, None])
    back_inner, back_state, back_step_size, back_gate_z, back_log_decay, back_skip_gain = scan_back(
        back_gated
    )
    (
        back_inner_raw,
        back_state_raw,
        back_step_raw,
        back_filter_inner,
        back_filter_state,
        back_step_bias,
    ) = mixer_back((back_inner, back_state, back_step_size))
    back_mixer_low = jnp.stack([back_gate_z, back_inner_raw], axis=1).astype(jnp.bfloat16)
    back_step_low = back_step_raw.astype(jnp.bfloat16)
    back_mixed_low = jnp.dot(back_mix, attention_all, preferred_element_type=jnp.float32).astype(
        jnp.bfloat16
    )
    back_attention_w = jnp.dot(back_mix.T, mixed_low, preferred_element_type=jnp.float32)
    back_query_rot, back_keys_rot, back_values = attend_back(
        query_low, keys_reduced, values_reduced, log_total, back_mixed_low, QB
    )
    back_query_low = (
        rotary_embed(back_query_rot, sequence_length, -1.0)
        .reshape(sequence_length, local_heads * HEAD_SIZE)
        .astype(jnp.bfloat16)
    )
    back_keys = rotary_embed(back_keys_rot[:, None, :], sequence_length, -1.0)[:, 0]
    select_heads = (jnp.arange(KEY_VALUE_HEADS) == head_group).astype(jnp.float32)
    pair = (
        jnp.stack([back_keys, back_values], axis=1)[:, :, None, :]
        * select_heads[None, None, :, None]
    )
    back_shared_part = jnp.concatenate(
        [pair.reshape(sequence_length, 2 * key_value_width), back_state_raw], axis=1
    )
    back_in_part = (
        jnp.dot(back_query_low, query_all.T, preferred_element_type=jnp.float32)
        + jnp.einsum(
            "scf,dcf->sd", back_mixer_low, mixer_in_all, preferred_element_type=jnp.float32
        )
        + jnp.dot(back_step_low, step_all.T, preferred_element_type=jnp.float32)
    )
    back_query_w = jnp.dot(seq_in.T, back_query_low, preferred_element_type=jnp.float32)
    back_mixer_in_w = jnp.einsum(
        "sd,scf->dcf", seq_in, back_mixer_low, preferred_element_type=jnp.float32
    )
    back_step_w = jnp.dot(seq_in.T, back_step_low, preferred_element_type=jnp.float32)
    back_in_rows, back_shared_rows = scatter_grads((back_in_part, back_shared_part))
    back_shared_low = back_shared_rows.astype(jnp.bfloat16)
    back_in_rows = back_in_rows + jnp.dot(
        back_shared_low, shared_all.T, preferred_element_type=jnp.float32
    )
    back_shared_w = jnp.dot(rows_in_low.T, back_shared_low, preferred_element_type=jnp.float32)
    back_gain_in = jnp.sum(back_in_rows * normed_in, axis=0)
    back_norm_in = back_in_rows * gain_in_all.astype(jnp.float32)
    back_inputs = back_hidden + scale_in * (
        back_norm_in - normed_in * jnp.mean(back_norm_in * normed_in, axis=1, keepdims=True)
    )
    back_gain_in, back_shared_w, back_filter_state, back_gain_post = (
        lax.psum(back_gain_in.astype(jnp.bfloat16), "tensor").astype(jnp.float32),
        lax.psum(back_shared_w.astype(jnp.bfloat16), "tensor").astype(jnp.float32),
        lax.psum(back_filter_state.astype(jnp.bfloat16), "tensor").astype(jnp.float32),
        lax.psum(back_gain_post.astype(jnp.bfloat16), "tensor").astype(jnp.float32),
    )
    (
        back_gain_in,
        back_query_w,
        back_shared_w,
        back_attention_w,
        back_mixer_in_w,
        back_step_w,
        back_filter_state,
        back_mixer_out_w,
        back_gain_post,
        back_gate_up_w,
        back_down_w,
    ) = (
        lax.psum_scatter(
            back_gain_in.astype(jnp.bfloat16), "dp", scatter_dimension=0, tiled=True
        ).astype(jnp.float32),
        lax.psum_scatter(
            back_query_w.astype(jnp.bfloat16), "dp", scatter_dimension=0, tiled=True
        ).astype(jnp.float32),
        lax.psum_scatter(
            back_shared_w.astype(jnp.bfloat16), "dp", scatter_dimension=0, tiled=True
        ).astype(jnp.float32),
        lax.psum_scatter(
            back_attention_w.astype(jnp.bfloat16), "dp", scatter_dimension=0, tiled=True
        ).astype(jnp.float32),
        lax.psum_scatter(
            back_mixer_in_w.astype(jnp.bfloat16), "dp", scatter_dimension=0, tiled=True
        ).astype(jnp.float32),
        lax.psum_scatter(
            back_step_w.astype(jnp.bfloat16), "dp", scatter_dimension=0, tiled=True
        ).astype(jnp.float32),
        lax.psum_scatter(
            back_filter_state.astype(jnp.bfloat16), "dp", scatter_dimension=0, tiled=True
        ).astype(jnp.float32),
        lax.psum_scatter(
            back_mixer_out_w.astype(jnp.bfloat16), "dp", scatter_dimension=0, tiled=True
        ).astype(jnp.float32),
        lax.psum_scatter(
            back_gain_post.astype(jnp.bfloat16), "dp", scatter_dimension=0, tiled=True
        ).astype(jnp.float32),
        lax.psum_scatter(
            back_gate_up_w.astype(jnp.bfloat16), "dp", scatter_dimension=0, tiled=True
        ).astype(jnp.float32),
        lax.psum_scatter(
            back_down_w.astype(jnp.bfloat16), "dp", scatter_dimension=0, tiled=True
        ).astype(jnp.float32),
    )
    back_filter_inner, back_step_bias, back_log_decay, back_skip_gain, back_mixer_gain = lax.psum(
        (back_filter_inner, back_step_bias, back_log_decay, back_skip_gain, back_mixer_gain), "dp"
    )
    return (
        output,
        back_inputs,
        back_gain_in,
        back_query_w,
        back_shared_w,
        back_attention_w,
        back_mixer_in_w,
        back_step_w,
        back_filter_inner,
        back_filter_state,
        back_step_bias,
        back_log_decay,
        back_skip_gain,
        back_mixer_gain,
        back_mixer_out_w,
        back_gain_post,
        back_gate_up_w,
        back_down_w,
    )


def solution(mesh):
    in_specs = (
        P(("dp", "tensor"), None),
        P(("dp", "tensor"), None),
        P("dp"),
        P("dp", "tensor"),
        P("dp", None),
        P("dp", "tensor"),
        P("dp", None, "tensor"),
        P("dp", "tensor"),
        P(None, "tensor"),
        P("dp", None),
        P("tensor"),
        P("tensor"),
        P("tensor"),
        P("tensor"),
        P("dp", "tensor"),
        P("dp"),
        P("dp", None, "tensor"),
        P("dp", "tensor"),
    )
    out_specs = (
        P(("dp", "tensor"), None),
        P(("dp", "tensor"), None),
        P("dp"),
        P("dp", "tensor"),
        P("dp", None),
        P("dp", "tensor"),
        P("dp", None, "tensor"),
        P("dp", "tensor"),
        P(None, "tensor"),
        P("dp", None),
        P("tensor"),
        P("tensor"),
        P("tensor"),
        P("tensor"),
        P("dp", "tensor"),
        P("dp"),
        P("dp", None, "tensor"),
        P("dp", "tensor"),
    )
    return jax.shard_map(body, mesh=mesh, in_specs=in_specs, out_specs=out_specs, check_vma=False)
```

profile of v0, /device:TPU:0, one launch (start us, length us, event | category | flops | bytes accessed | tf_op | source)
XLA Modules:
  0.0 1368.5 jit_solution(16350815531846040670)
XLA Ops:
  8.0 22.3 %all-gather = bf16[8,1,128]{2,1,0:T(2,128)(2,1)S(1)} all-gather(bf16[1,1,128]{2,1,0:T(2,128)(2,1)} %bitcast.481), channel_id=1, replica_groups=mesh['dp'=8,'tensor'=4] {'dp'}, dimensions={0}, use_global_device_ids=true | all-gather | bytes 2304 | tf_op jit(solution)/shard_map/all_gather | solution.py:234
  35.1 26.1 %all-gather.1 = bf16[8,32,5]{1,2,0:T(8,128)(2,1)S(1)} all-gather(bf16[1,32,5]{1,2,0:T(8,128)(2,1)S(1)} %bitcast.480), channel_id=1, replica_groups=mesh['dp'=8,'tensor'=4] {'dp'}, dimensions={0}, use_global_device_ids=true | all-gather | bytes 2880 | tf_op jit(solution)/shard_map/all_gather | solution.py:240
  61.5 32.9 %all_gather.57 = bf16[1024,128]{1,0:T(8,128)(2,1)} all-gather(bf16[128,128]{1,0:T(8,128)(2,1)S(1)} %copy-done.83), channel_id=1, replica_groups=mesh['dp'=8,'tensor'=4] {'dp'}, dimensions={0}, use_global_device_ids=true | all-gather | bytes 294912 | tf_op jit(solution)/shard_map/all_gather | solution.py:235
  95.7 33.4 %all_gather.59 = bf16[1024,128]{1,0:T(8,128)(2,1)} all-gather(bf16[128,128]{1,0:T(8,128)(2,1)S(1)} %copy-done.84), channel_id=1, replica_groups=mesh['dp'=8,'tensor'=4] {'dp'}, dimensions={0}, use_global_device_ids=true | all-gather | bytes 294912 | tf_op jit(solution)/shard_map/all_gather | solution.py:237
  129.1 33.9 %all_gather.63 = bf16[1024,384]{1,0:T(8,128)(2,1)} all-gather(bf16[128,384]{1,0:T(8,128)(2,1)S(1)} %copy-done.78), channel_id=1, replica_groups=mesh['dp'=8,'tensor'=4] {'dp'}, dimensions={0}, use_global_device_ids=true | all-gather | bytes 884736 | tf_op jit(solution)/shard_map/all_gather | solution.py:241
  163.4 26.0 %all_gather.62 = bf16[1024,6]{0,1:T(8,128)(2,1)S(1)} all-gather(bf16[128,6]{0,1:T(8,128)(2,1)S(1)} %copy-done.139), channel_id=1, replica_groups=mesh['dp'=8,'tensor'=4] {'dp'}, dimensions={0}, use_global_device_ids=true | all-gather | bytes 13824 | tf_op jit(solution)/shard_map/all_gather | solution.py:239
  190.8 2.9 fusion.133
  203.1 4.4 multiply_convert_fusion.7
  208.3 3.3 fusion.62
  221.4 18.4 %while.63 = (s32[]{:T(128)}, f32[6,64,128]{2,1,0:T(8,128)S(1)}, f32[8,6,64,128]{3,2,1,0:T(8,128)}, f32[8,6,1,1]{1,3,2,0:T(1,128)}, f32[8,6]{1,0:T(8,128)S(1)}, /...) while((s32[]{:T(128)}, f32[6,64,128]{2,1,0:T(8,128)S(1)}, f32[8,6,64,128]{3,2,1,0:T(8,128)}, ...), condition=%wide.region_7.8_spmd.clone, body=%wide.region_6.7_spmd.clone.sunk | while | flops 196611 | bytes 984776 | solution.py:97
  243.9 3.5 bitcast_add_fusion.4
  249.8 3.2 copy.219
  253.0 3.6 multiply_reduce_fusion.9
  256.6 5.8 psum.77
  266.8 12.6 while.62
  285.9 16.2 %all-gather.2 = bf16[8,1,128]{2,1,0:T(2,128)(2,1)S(1)} all-gather(bf16[1,1,128]{2,1,0:T(2,128)(2,1)S(1)} %bitcast.482), channel_id=1, replica_groups=mesh['dp'=8,'tensor'=4] {'dp'}, dimensions={0}, use_global_device_ids=true | all-gather | bytes 2304 | tf_op jit(solution)/shard_map/all_gather | solution.py:242
  302.1 11.4 reduce-scatter.21.cloned.1.call-done
  318.4 47.2 %all-gather.20.cloned.1.call-done = bf16[1024,2,512]{2,0,1:T(8,128)(2,1)} async-done(((bf16[128,2,512]{2,0,1:T(8,128)(2,1)}), bf16[1024,2,512]{2,0,1:T(8,128)(2,1)}) %all-gather.20.cloned.1.call-update) | async-done | bytes 2097168 | tf_op jit(solution)/shard_map/all_gather | solution.py:243
  365.6 23.2 %all-gather.18.cloned.1.call-done = bf16[1024,1024]{1,0:T(8,128)(2,1)} async-done(((bf16[256,1024]{1,0:T(8,128)(2,1)}), bf16[1024,1024]{1,0:T(8,128)(2,1)}) %all-gather.18.cloned.1.call-update) | async-done | bytes 2097168 | tf_op jit(solution)/shard_map/all_gather | solution.py:186
  388.8 6.5 fusion.58
  395.3 36.1 %all-gather.22.cloned.1.call-done = bf16[1024,512]{1,0:T(8,128)(2,1)} async-done(((bf16[128,512]{1,0:T(8,128)(2,1)}), bf16[1024,512]{1,0:T(8,128)(2,1)}) %all-gather.22.cloned.1.call-update) | async-done | bytes 1048592 | tf_op jit(solution)/shard_map/all_gather | solution.py:244
  431.4 23.0 %all-gather.24.cloned.1.call-done = bf16[1024,1024]{1,0:T(8,128)(2,1)} async-done(((bf16[256,1024]{1,0:T(8,128)(2,1)}), bf16[1024,1024]{1,0:T(8,128)(2,1)}) %all-gather.24.cloned.1.call-update) | async-done | bytes 2097168 | tf_op jit(solution)/shard_map/all_gather | solution.py:186
  454.4 6.4 fusion.129
  462.1 3.7 bitcast_convert_fusion
  465.9 31.5 %reduce-scatter.25.cloned.1.call-done = bf16[256,1024]{1,0:T(8,128)(2,1)} async-done(((bf16[1024,1024]{1,0:T(8,128)(2,1)}), bf16[256,1024]{1,0:T(8,128)(2,1)}) %reduce-scatter.25.cloned.1.call-update) | async-done | bytes 524304 | tf_op jit(solution)/shard_map/reduce_scatter | solution.py:196
  503.0 21.7 %all-gather.26.cloned.1.call-done = bf16[1024,1024]{1,0:T(8,128)(2,1)} async-done(((bf16[256,1024]{1,0:T(8,128)(2,1)}), bf16[1024,1024]{1,0:T(8,128)(2,1)}) %all-gather.26.cloned.1.call-update) | async-done | bytes 2097168 | tf_op jit(solution)/shard_map/all_gather | solution.py:186
  524.7 4.9 multiply_reduce_fusion.2
  529.6 5.9 psum.78
  535.4 5.1 fusion.74
  546.3 3.6 fusion.113
  551.3 20.5 %while.65 = (s32[]{:T(128)}, f32[6,64,128]{2,1,0:T(8,128)S(1)}, f32[8,6]{1,0:T(8,128)S(1)}, f32[8,6,64,128]{3,2,1,0:T(8,128)}, f32[8,6,64,128]{3,2,1,0:T(8,128)}...) while((s32[]{:T(128)}, f32[6,64,128]{2,1,0:T(8,128)S(1)}, ...), condition=%wide.region_22.23_spmd.clone, body=%wide.region_20.22_spmd.clone.sunk | while | flops 294910 | bytes 1179932 | solution.py:97
  572.4 7.3 fusion.69
  585.9 42.5 %while.64 = (s32[]{:T(128)}, f32[1024,64]{0,1:T(8,128)}, f32[1024,64]{0,1:T(8,128)}, f32[2,512,2,64]{1,0,3,2:T(2,128)}, s32[2]{0:T(128)S(1)}, /*index=5*/bf16[10...) while((s32[]{:T(128)}, f32[1024,64]{0,1:T(8,128)}, ...), condition=%wide.region_17.18_spmd.clone, body=%wide.region_15.17_spmd.clone.sunk | while | flops 682491392 | bytes 57303528 | solution.py:179
  588.4 3.4 fusion.292
  595.7 5.8 dynamic_update_slice.61
  603.6 2.8 fusion.295
  609.5 3.4 fusion.292
  616.8 5.8 dynamic_update_slice.61
  624.8 2.8 fusion.295
  634.7 3.0 multiply_reduce_fusion.12
  641.0 2.9 fusion.109
  645.4 5.7 fusion.65
  677.3 3.1 convolution_convert_fusion.4
  680.7 5.7 bitcast_add_fusion.3
  688.8 3.1 copy.227
  691.9 4.3 convolution_convert_fusion.3
  696.2 5.1 multiply_reduce_fusion.5
  703.3 3.0 fusion.70
  712.8 3.2 fusion.48
  722.0 11.7 reduce-scatter.45.cloned.1.call-done
  735.6 68.4 %reduce-scatter.39.cloned.1.call-done = bf16[128,2,512]{2,0,1:T(8,128)(2,1)} async-done(((bf16[1024,2,512]{2,0,1:T(8,128)(2,1)}), bf16[128,2,512]{2,0,1:T(8,128)(2,1)}) %reduce-scatter.39.cloned.1.call-update) | async-done | bytes 262160 | tf_op jit(solution)/shard_map/reduce_scatter | solution.py:483
  806.4 35.5 %all-reduce.28 = (f32[5,384]{1,0:T(8,128)}, f32[6]{0:T(128)}, f32[6]{0:T(128)}, f32[6]{0:T(128)}, f32[384]{0:T(512)}) all-reduce(f32[5,384]{1,0:T(8,128)S(1)} %pad_add_fusion.6, f32[6]{0:T(128)S(1)} %copy-done.137, f32[6]{0:T(128)S(1)} %negate_multiply_fusion, f32[6]{0:T(128)S(1)} %reduce_sum.339, ...), channel_id=1, replica_groups=mesh['dp'=8,'tensor'=4] {'dp'}, use_global_device_ids=true, to_apply=%region_47.48 | all-reduce | flops 2322 | bytes 18576 | tf_op jit(solution)/shard_map/psum | solution.py:490
  841.9 26.2 %reduce-scatter.47.cloned.1.call-done = bf16[32,5]{1,0:T(8,128)(2,1)} async-done(((bf16[256,5]{1,0:T(8,128)(2,1)}), bf16[32,5]{1,0:T(8,128)(2,1)}) %reduce-scatter.47.cloned.1.call-update) | async-done | bytes 336
  868.9 63.3 %reduce-scatter.43.cloned.1.call-done = bf16[128,6]{1,0:T(8,128)(2,1)} async-done(((bf16[1024,6]{1,0:T(8,128)(2,1)}), bf16[128,6]{1,0:T(8,128)(2,1)}) %reduce-scatter.43.cloned.1.call-update) | async-done | bytes 1552
  933.6 62.6 %reduce-scatter.31.cloned.1.call-done = bf16[128,128]{1,0:T(8,128)(2,1)} async-done(((bf16[1024,128]{1,0:T(8,128)(2,1)}), bf16[128,128]{1,0:T(8,128)(2,1)}) %reduce-scatter.31.cloned.1.call-update) | async-done | bytes 32784 | tf_op jit(solution)/shard_map/reduce_scatter | solution.py:459
  997.6 62.6 %reduce-scatter.33.cloned.1.call-done = bf16[128,128]{1,0:T(8,128)(2,1)} async-done(((bf16[1024,128]{1,0:T(8,128)(2,1)}), bf16[128,128]{1,0:T(8,128)(2,1)}) %reduce-scatter.33.cloned.1.call-update) | async-done | bytes 32784 | tf_op jit(solution)/shard_map/reduce_scatter | solution.py:465
  1061.6 63.2 %reduce-scatter.37.cloned.1.call-done = bf16[128,384]{1,0:T(8,128)(2,1)} async-done(((bf16[1024,384]{1,0:T(8,128)(2,1)}), bf16[128,384]{1,0:T(8,128)(2,1)}) %reduce-scatter.37.cloned.1.call-update) | async-done | bytes 98320 | tf_op jit(solution)/shard_map/reduce_scatter | solution.py:477
  1126.5 66.2 %reduce-scatter.35.cloned.1.call-done = bf16[128,2,384]{2,0,1:T(8,128)(2,1)} async-done(((bf16[1024,2,384]{2,0,1:T(8,128)(2,1)}), bf16[128,2,384]{2,0,1:T(8,128)(2,1)}) %reduce-scatter.35.cloned.1.call-update) | async-done | bytes 196624 | tf_op jit(solution)/shard_map/reduce_scatter | solution.py:468
  1194.5 64.4 %reduce-scatter.41.cloned.1.call-done = bf16[128,512]{1,0:T(8,128)(2,1)} async-done(((bf16[1024,512]{1,0:T(8,128)(2,1)}), bf16[128,512]{1,0:T(8,128)(2,1)}) %reduce-scatter.41.cloned.1.call-update) | async-done | bytes 131088 | tf_op jit(solution)/shard_map/reduce_scatter | solution.py:462
  1259.0 33.1 %reduce-scatter.27.cloned.1.call-done = bf16[256,1024]{1,0:T(8,128)(2,1)} async-done(((bf16[1024,1024]{1,0:T(8,128)(2,1)}), bf16[256,1024]{1,0:T(8,128)(2,1)}) %reduce-scatter.27.cloned.1.call-update) | async-done | bytes 524304 | tf_op jit(solution)/shard_map/reduce_scatter | solution.py:196
  1294.7 31.3 %reduce-scatter.23.cloned.1.call-done = bf16[256,1024]{1,0:T(8,128)(2,1)} async-done(((bf16[1024,1024]{1,0:T(8,128)(2,1)}), bf16[256,1024]{1,0:T(8,128)(2,1)}) %reduce-scatter.23.cloned.1.call-update) | async-done | bytes 524304 | tf_op jit(solution)/shard_map/reduce_scatter | solution.py:190
  1326.1 3.2 fusion.122
  1329.3 21.4 %all-reduce.29 = (bf16[1024]{0:T(1024)(128)(2,1)S(1)}, bf16[1024]{0:T(1024)(128)(2,1)S(1)}) all-reduce(bf16[1024]{0:T(1024)(128)(2,1)S(1)} %get-tuple-element.589, bf16[1024]{0:T(1024)(128)(2,1)S(1)} %copy-done.127), channel_id=7, replica_groups=mesh['dp'=8,'tensor'=4] {'dp'}, use_global_device_ids=true, to_apply=%region_35.36.clone | all-reduce | flops 2048 | bytes 8192
  1350.8 5.9 all-reduce.30
  (636 shorter events, 210.7 us)
Async XLA Ops:
  7.2 54.2 %copy-start.149 = (bf16[6]{0:T(256)(128)(2,1)S(1)}, bf16[6]{0:T(256)(128)(2,1)}, u32[]{:S(2)}) copy-start(bf16[6]{0:T(256)(128)(2,1)} %param.37) | copy-start | bytes 40
  7.2 54.2 %copy-start.129 = (bf16[5,384]{1,0:T(8,128)(2,1)S(1)}, bf16[5,384]{1,0:T(8,128)(2,1)}, u32[]{:S(2)}) copy-start(bf16[5,384]{1,0:T(8,128)(2,1)} %param.34) | copy-start | bytes 11524
  7.2 54.3 %copy-start.83 = (bf16[128,128]{1,0:T(8,128)(2,1)S(1)}, bf16[128,128]{1,0:T(8,128)(2,1)}, u32[]{:S(2)}) copy-start(bf16[128,128]{1,0:T(8,128)(2,1)} %param.29) | copy-start | bytes 98308
  7.2 182.2 %all-gather.14.cloned.1.call-start = ((), (), s32[]{:S(2)}) async-start(), calls=%async_computation.15 | async-start | bytes 1179648 | tf_op jit(solution)/shard_map/all_gather | solution.py:236
  8.0 182.8 %all-gather.12.cloned.1.call-start = ((), (), s32[]{:S(2)}) async-start(), calls=%async_computation.14 | async-start | bytes 2621440 | tf_op jit(solution)/shard_map/all_gather | solution.py:186
  31.6 64.1 %copy-start.84 = (bf16[128,128]{1,0:T(8,128)(2,1)S(1)}, bf16[128,128]{1,0:T(8,128)(2,1)}, u32[]{:S(2)}) copy-start(bf16[128,128]{1,0:T(8,128)(2,1)} %param.31) | copy-start | bytes 98308
  32.2 97.0 %copy-start.78 = (bf16[128,384]{1,0:T(8,128)(2,1)S(1)}, bf16[128,384]{1,0:T(8,128)(2,1)}, u32[]{:S(2)}) copy-start(bf16[128,384]{1,0:T(8,128)(2,1)} %param.40) | copy-start | bytes 294916
  34.2 129.0 %copy-start.148 = (bf16[6]{0:T(256)(128)(2,1)S(1)}, bf16[6]{0:T(256)(128)(2,1)}, u32[]{:S(2)}) copy-start(bf16[6]{0:T(256)(128)(2,1)} %param.36) | copy-start | bytes 40
  34.2 129.0 %copy-start.143 = (bf16[6]{0:T(256)(128)(2,1)S(1)}, bf16[6]{0:T(256)(128)(2,1)}, u32[]{:S(2)}) copy-start(bf16[6]{0:T(256)(128)(2,1)} %param.38) | copy-start | bytes 40
  34.2 129.1 %copy-start.141 = (bf16[384]{0:T(512)(128)(2,1)S(1)}, bf16[384]{0:T(512)(128)(2,1)}, u32[]{:S(2)}) copy-start(bf16[384]{0:T(512)(128)(2,1)} %param.39) | copy-start | bytes 2308
  34.2 129.2 %copy-start.139 = (bf16[128,6]{0,1:T(8,128)(2,1)S(1)}, bf16[128,6]{0,1:T(8,128)(2,1)}, u32[]{:S(2)}) copy-start(bf16[128,6]{0,1:T(8,128)(2,1)} %param.33) | copy-start | bytes 4612
  34.3 174.0 %all-gather.16.cloned.1.call-start = ((), (), s32[]{:S(2)}) async-start(), calls=%async_computation.16 | async-start | bytes 1769472 | tf_op jit(solution)/shard_map/all_gather | solution.py:238
  35.0 278.4 %reduce-scatter.21.cloned.1.call-start = ((), (), s32[]{:S(2)}) async-start(), calls=%async_computation.17 | async-start | bytes 2621440 | tf_op jit(solution)/shard_map/reduce_scatter | solution.py:190
  35.1 228.5 %copy-start.130 = (f32[32]{0:T(128)}, f32[32]{0:T(128)S(1)}, u32[]{:S(2)}) copy-start(f32[32]{0:T(128)S(1)} %multiply_power_fusion) | copy-start | bytes 388
  61.4 141.7 %copy-start.119 = (f32[1,256]{1,0:T(1,128)}, f32[1,256]{1,0:T(1,128)S(1)}, u32[]{:S(2)}) copy-start(f32[1,256]{1,0:T(1,128)S(1)} %get-tuple-element.723) | copy-start | bytes 3076
  61.4 141.7 %copy-start.121 = (f32[1,256]{1,0:T(1,128)}, f32[1,256]{1,0:T(1,128)S(1)}, u32[]{:S(2)}) copy-start(f32[1,256]{1,0:T(1,128)S(1)} %get-tuple-element.724) | copy-start | bytes 3076
  61.4 141.7 %copy-start.123 = (f32[1,256]{1,0:T(1,128)}, f32[1,256]{1,0:T(1,128)S(1)}, u32[]{:S(2)}) copy-start(f32[1,256]{1,0:T(1,128)S(1)} %get-tuple-element.725) | copy-start | bytes 3076
  61.4 141.7 %copy-start.125 = (f32[1,256]{1,0:T(1,128)}, f32[1,256]{1,0:T(1,128)S(1)}, u32[]{:S(2)}) copy-start(f32[1,256]{1,0:T(1,128)S(1)} %get-tuple-element.726) | copy-start | bytes 3076
  61.4 135.7 %copy-start.135 = (f32[6]{0:T(128)}, f32[6]{0:T(128)S(1)}, u32[]{:S(2)}) copy-start(f32[6]{0:T(128)S(1)} %fusion.174) | copy-start | bytes 76
  61.5 151.8 %copy-start.99 = (f32[384]{0:T(512)}, f32[384]{0:T(512)S(1)}, u32[]{:S(2)}) copy-start(f32[384]{0:T(512)S(1)} %get-tuple-element.596) | copy-start | bytes 4612
  61.5 151.8 %copy-start.101 = (f32[384]{0:T(512)}, f32[384]{0:T(512)S(1)}, u32[]{:S(2)}) copy-start(f32[384]{0:T(512)S(1)} %get-tuple-element.597) | copy-start | bytes 4612
  61.5 151.8 %copy-start.103 = (f32[384]{0:T(512)}, f32[384]{0:T(512)S(1)}, u32[]{:S(2)}) copy-start(f32[384]{0:T(512)S(1)} %get-tuple-element.598) | copy-start | bytes 4612
  61.5 151.8 %copy-start.105 = (f32[384]{0:T(512)}, f32[384]{0:T(512)S(1)}, u32[]{:S(2)}) copy-start(f32[384]{0:T(512)S(1)} %get-tuple-element.599) | copy-start | bytes 4612
  163.1 80.7 %copy-start.112 = (pred[128,128]{1,0:T(8,128)(4,1)}, pred[128,128]{1,0:T(8,128)(4,1)S(1)}, u32[]{:S(2)}) copy-start(pred[128,128]{1,0:T(8,128)(4,1)S(1)} %iota_compare_fusion.2) | copy-start | bytes 49156
  163.4 89.6 %copy-start.94 = (f32[384]{0:T(512)}, f32[384]{0:T(512)S(1)}, u32[]{:S(2)}) copy-start(f32[384]{0:T(512)S(1)} %mul.913) | copy-start | bytes 4612
  163.4 117.2 %copy-start.107 = (f32[384]{0:T(512)}, f32[384]{0:T(512)S(1)}, u32[]{:S(2)}) copy-start(f32[384]{0:T(512)S(1)} %convert_element_type.222) | copy-start | bytes 4612
  197.8 46.1 %copy-start.91 = (f32[8,128,6]{1,2,0:T(8,128)}, f32[8,128,6]{1,2,0:T(8,128)S(1)}, u32[]{:S(2)}) copy-start(f32[8,128,6]{1,2,0:T(8,128)S(1)} %get-tuple-element.720) | copy-start | bytes 73732
  200.7 43.2 %copy-start.85 = (f32[8,128,6]{1,2,0:T(8,128)}, f32[8,128,6]{1,2,0:T(8,128)S(1)}, u32[]{:S(2)}) copy-start(f32[8,128,6]{1,2,0:T(8,128)S(1)} %copy.210) | copy-start | bytes 73732
  208.3 35.2 %copy-start.26 = (bf16[1024,128]{1,0:T(8,128)(2,1)}, bf16[1024,128]{1,0:T(8,128)(2,1)S(1)}, u32[]{:S(2)}) copy-start(bf16[1024,128]{1,0:T(8,128)(2,1)S(1)} %get-tuple-element.713) | copy-start | bytes 786436
  284.2 29.3 %copy-start.3 = (bf16[256,1024]{1,0:T(8,128)(2,1)S(1)}, bf16[256,1024]{1,0:T(8,128)(2,1)}, u32[]{:S(2)}) copy-start(bf16[256,1024]{1,0:T(8,128)(2,1)} %param.26) | copy-start | bytes 1572868
  284.2 81.4 %all-gather.20.cloned.1.call-start = ((), (), s32[]{:S(2)}) async-start(), calls=%async_computation.19 | async-start | bytes 2359296 | tf_op jit(solution)/shard_map/all_gather | solution.py:243
  285.9 102.9 %all-gather.18.cloned.1.call-start = ((), (), s32[]{:S(2)}) async-start(), calls=%async_computation.18 | async-start | bytes 2621440 | tf_op jit(solution)/shard_map/all_gather | solution.py:186
  314.8 184.9 %copy-start.97 = (f32[256]{0:T(256)}, f32[256]{0:T(256)S(1)}, u32[]{:S(2)}) copy-start(f32[256]{0:T(256)S(1)} %add_rsqrt_fusion.1) | copy-start | bytes 3076
  316.8 114.5 %all-gather.22.cloned.1.call-start = ((), (), s32[]{:S(2)}) async-start(), calls=%async_computation.20 | async-start | bytes 1179648 | tf_op jit(solution)/shard_map/all_gather | solution.py:244
  317.6 136.8 %all-gather.24.cloned.1.call-start = ((), (), s32[]{:S(2)}) async-start(), calls=%async_computation.22 | async-start | bytes 2621440 | tf_op jit(solution)/shard_map/all_gather | solution.py:186
  318.3 179.1 %reduce-scatter.25.cloned.1.call-start = ((), (), s32[]{:S(2)}) async-start(), calls=%async_computation.23 | async-start | bytes 2621440 | tf_op jit(solution)/shard_map/reduce_scatter | solution.py:196
  465.8 31.6 %copy-start.14 = (bf16[256,1024]{1,0:T(8,128)(2,1)S(1)}, bf16[256,1024]{1,0:T(8,128)(2,1)}, u32[]{:S(2)}) copy-start(bf16[256,1024]{1,0:T(8,128)(2,1)} %reduce-scatter.21.cloned.1.call-done) | copy-start | bytes 1572868
  465.9 58.9 %all-gather.26.cloned.1.call-start = ((), (), s32[]{:S(2)}) async-start(), calls=%async_computation.24 | async-start | bytes 2621440 | tf_op jit(solution)/shard_map/all_gather | solution.py:186
  502.0 204.4 %reduce-scatter.29.cloned.1.call-start = ((), (), s32[]{:S(2)}) async-start(), calls=%async_computation.26 | async-start | bytes 1310720 | tf_op jit(solution)/shard_map/reduce_scatter | solution.py:196
  503.0 32.5 %copy-start.95 = (f32[384]{0:T(512)S(1)}, f32[384]{0:T(512)}, u32[]{:S(2)}) copy-start(f32[384]{0:T(512)} %copy-done.94) | copy-start | bytes 4612
  640.5 93.3 %reduce-scatter.45.cloned.1.call-start = ((), (), s32[]{:S(2)}) async-start(), calls=%async_computation.35 | async-start | bytes 1179648
  645.3 158.8 %reduce-scatter.39.cloned.1.call-start = ((), (), s32[]{:S(2)}) async-start(), calls=%async_computation.31 | async-start | bytes 2359296 | tf_op jit(solution)/shard_map/reduce_scatter | solution.py:483
  651.1 217.1 %reduce-scatter.47.cloned.1.call-start = ((), (), s32[]{:S(2)}) async-start(), calls=%async_computation.36 | async-start | bytes 73728
  671.5 260.7 %reduce-scatter.43.cloned.1.call-start = ((), (), s32[]{:S(2)}) async-start(), calls=%async_computation.34 | async-start | bytes 294912
  674.7 321.6 %reduce-scatter.31.cloned.1.call-start = ((), (), s32[]{:S(2)}) async-start(), calls=%async_computation.27 | async-start | bytes 294912 | tf_op jit(solution)/shard_map/reduce_scatter | solution.py:459
  677.3 383.0 %reduce-scatter.33.cloned.1.call-start = ((), (), s32[]{:S(2)}) async-start(), calls=%async_computation.28 | async-start | bytes 294912 | tf_op jit(solution)/shard_map/reduce_scatter | solution.py:465
  680.4 444.5 %reduce-scatter.37.cloned.1.call-start = ((), (), s32[]{:S(2)}) async-start(), calls=%async_computation.30 | async-start | bytes 884736 | tf_op jit(solution)/shard_map/reduce_scatter | solution.py:477
  696.1 496.5 %reduce-scatter.35.cloned.1.call-start = ((), (), s32[]{:S(2)}) async-start(), calls=%async_computation.29 | async-start | bytes 1769472 | tf_op jit(solution)/shard_map/reduce_scatter | solution.py:468
  706.3 552.6 %reduce-scatter.41.cloned.1.call-start = ((), (), s32[]{:S(2)}) async-start(), calls=%async_computation.32 | async-start | bytes 1179648 | tf_op jit(solution)/shard_map/reduce_scatter | solution.py:462
  709.8 582.3 %reduce-scatter.27.cloned.1.call-start = ((), (), s32[]{:S(2)}) async-start(), calls=%async_computation.25 | async-start | bytes 2621440 | tf_op jit(solution)/shard_map/reduce_scatter | solution.py:196
  716.0 610.0 %reduce-scatter.23.cloned.1.call-start = ((), (), s32[]{:S(2)}) async-start(), calls=%async_computation.21 | async-start | bytes 2621440 | tf_op jit(solution)/shard_map/reduce_scatter | solution.py:190
  720.1 86.0 %copy-start.128 = (f32[384]{0:T(512)S(1)}, f32[384]{0:T(512)}, u32[]{:S(2)}) copy-start(f32[384]{0:T(512)} %get-tuple-element.670) | copy-start | bytes 4612
  720.1 86.2 %copy-start.142 = (f32[6]{0:T(128)S(1)}, f32[6]{0:T(128)}, u32[]{:S(2)}) copy-start(f32[6]{0:T(128)} %get-tuple-element.719) | copy-start | bytes 76
  720.1 86.2 %copy-start.150 = (bf16[6]{0:T(256)(128)(2,1)S(1)}, bf16[6]{0:T(256)(128)(2,1)}, u32[]{:S(2)}) copy-start(bf16[6]{0:T(256)(128)(2,1)} %param.37) | copy-start | bytes 40
  720.1 86.2 %copy-start.137 = (f32[6]{0:T(128)S(1)}, f32[6]{0:T(128)}, u32[]{:S(2)}) copy-start(f32[6]{0:T(128)} %get-tuple-element.672) | copy-start | bytes 76
  720.1 86.2 %copy-start.140 = (f32[384]{0:T(512)S(1)}, f32[384]{0:T(512)}, u32[]{:S(2)}) copy-start(f32[384]{0:T(512)} %get-tuple-element.579) | copy-start | bytes 4612
  720.2 571.9 %copy-start.55 = (bf16[1024,512]{1,0:T(8,128)(2,1)S(1)}, bf16[1024,512]{1,0:T(8,128)(2,1)}, u32[]{:S(2)}) copy-start(bf16[1024,512]{1,0:T(8,128)(2,1)} %all-gather.14.cloned.1.call-done) | copy-start | bytes 3145732
  720.2 571.9 %copy-start.82 = (f32[8,1,128]{2,1,0:T(1,128)S(1)}, f32[8,1,128]{2,1,0:T(1,128)}, u32[]{:S(2)}) copy-start(f32[8,1,128]{2,1,0:T(1,128)} %copy-done.81) | copy-start | bytes 12292
  720.2 571.9 %copy-start.116 = (f32[256]{0:T(256)S(1)}, f32[256]{0:T(256)}, u32[]{:S(2)}) copy-start(f32[256]{0:T(256)} %copy-done.115) | copy-start | bytes 3076
  720.2 639.7 %all-reduce.33.cloned.1.call-start = ((), (), s32[]{:S(2)}) async-start(), calls=%async_computation.33 | async-start | bytes 262144 | tf_op jit(solution)/shard_map/psum | solution.py:439
  1258.9 67.1 %copy-start.36 = (bf16[256,1024]{1,0:T(8,128)(2,1)S(1)}, bf16[256,1024]{1,0:T(8,128)(2,1)}, u32[]{:S(2)}) copy-start(bf16[256,1024]{1,0:T(8,128)(2,1)} %reduce-scatter.25.cloned.1.call-done) | copy-start | bytes 1572868
  1258.9 67.1 %copy-start.37 = (bf16[256,1024]{1,0:T(8,128)(2,1)S(1)}, bf16[256,1024]{1,0:T(8,128)(2,1)}, u32[]{:S(2)}) copy-start(bf16[256,1024]{1,0:T(8,128)(2,1)} %param.27) | copy-start | bytes 1572868
  1258.9 67.1 %copy-start.98 = (f32[256]{0:T(256)S(1)}, f32[256]{0:T(256)}, u32[]{:S(2)}) copy-start(f32[256]{0:T(256)} %copy-done.97) | copy-start | bytes 3076
  1259.0 67.1 %copy-start.118 = (f32[256]{0:T(256)S(1)}, f32[256]{0:T(256)}, u32[]{:S(2)}) copy-start(f32[256]{0:T(256)} %copy-done.117) | copy-start | bytes 3076
  (124 other events, 546.9 us)
Sparse Core Ops, SparseCore 0:
  10.2 43.0 all-gather.13
  55.4 21.3 all-gather.11
  79.5 49.4 all-gather.15
  284.3 29.1 reduce-scatter.20
  316.3 49.2 all-gather.19
  367.7 21.0 all-gather.17
  391.1 40.2 all-gather.21
  433.0 21.3 all-gather.23
  466.0 31.4 reduce-scatter.24
  502.1 22.5 all-gather.25
  640.6 25.9 reduce-scatter.28
  670.2 63.4 reduce-scatter.44
  737.3 66.7 reduce-scatter.38
  807.9 60.2 reduce-scatter.46
  871.9 60.2 reduce-scatter.42
  935.9 60.2 reduce-scatter.30
  1000.0 60.2 reduce-scatter.32
  1063.4 61.4 reduce-scatter.36
  1128.7 63.9 reduce-scatter.34
  1196.5 62.3 reduce-scatter.40
  1261.6 30.4 reduce-scatter.26
  1294.6 31.4 reduce-scatter.22
  1328.5 31.4 all-reduce.32
where the time goes:
time: 1380 us; the launch traced here: 1370 us
  waiting for transfers between devices  751 us (54%)
  blocking collectives  265 us (19%)
  matrix products  130 us (9%)
  local copies, waits for them, and re-layouts  100 us (7%)
  other arithmetic  98.7 us (7%)
  between operations  17.1 us (1%)
    unnamed x26, waiting for transfers between devices  104 us
    reduce_scatter x1, waiting for transfers between devices, body(): lax.psum_scatter(back_gate_up_w.astype(jnp.bfloat16), 'dp', scatter_dimen...  68.4 us
    all_gather x4, waiting for transfers between devices, gather_rows(): return lax.all_gather(values, 'tensor', axis=0, tiled=True)  68 us
    reduce_scatter x1, waiting for transfers between devices, body(): lax.psum_scatter(back_mixer_in_w.astype(jnp.bfloat16), 'dp', scatter_dime...  66.2 us
    reduce_scatter x3, waiting for transfers between devices, scatter_grads(): lax.psum_scatter(as_sent(values), 'tensor', scatter_dimension=0, tiled=True)  64.6 us
    reduce_scatter x1, waiting for transfers between devices, body(): lax.psum_scatter(back_shared_w.astype(jnp.bfloat16), 'dp', scatter_dimens...  64.4 us
    reduce_scatter x1, waiting for transfers between devices, body(): lax.psum_scatter(back_mixer_out_w.astype(jnp.bfloat16), 'dp', scatter_dim...  63.2 us
    reduce_scatter x1, waiting for transfers between devices, body(): lax.psum_scatter(back_query_w.astype(jnp.bfloat16), 'dp', scatter_dimensi...  62.6 us
  transfers between devices with their start and end apart: 23, of which 19 were waited for; matrix products, arithmetic and copies ran while one was open for 9% of the time, Pallas kernels for 0%

commit v1 on v0

v1 whole, which is shorter than its diff:
```python
import jax
import jax.numpy as jnp
from jax import lax
from jax.sharding import PartitionSpec as P

QUERY_HEADS = 8
HEAD_SIZE = 64
KEY_VALUE_HEADS = 2
NH = 24
PH = 64
BLK = 128
QB = 512


epsilon = 1e-05
rope_base = 100000000000.0
highest_precision = lax.Precision.HIGHEST


def as_sent(x):

    def short(part):
        return part.astype(jnp.bfloat16) if part.dtype == jnp.float32 else part

    return jax.tree.map(short, x)


def norm_scale(values):
    return lax.rsqrt(jnp.mean(values * values, axis=-1, keepdims=True) + epsilon)


def rotary_embed(values, sequence_length, sign):
    half = values.shape[-1] // 2
    position = jnp.arange(sequence_length, dtype=jnp.float32)
    frequency = rope_base ** (-jnp.arange(half, dtype=jnp.float32) * 2.0 / values.shape[-1])
    angle = position[:, None] * frequency[None, :]
    cosine = jnp.cos(angle)[:, None, :]
    sine = sign * jnp.sin(angle)[:, None, :]
    first = values[..., :half]
    second = values[..., half:]
    return jnp.concatenate(
        [first * cosine - second * sine, second * cosine + first * sine], axis=-1
    )


def causal_filter(values, taps, bias):
    width = taps.shape[0]
    sequence_length = values.shape[0]
    padded = jnp.pad(values, ((width - 1, 0), (0, 0)))
    total = bias[None, :] + jnp.zeros_like(values)
    for offset in range(width):
        total = total + taps[offset][None, :] * padded[offset : offset + sequence_length]
    return total


def mixer_input(inner_raw, state_raw, step_raw, filter_inner, filter_state, step_bias):
    kernel = filter_inner.shape[0] - 1
    inner = jax.nn.silu(causal_filter(inner_raw, filter_inner[:kernel], filter_inner[kernel]))
    state_in = jax.nn.silu(
        causal_filter(state_raw, jnp.transpose(filter_state[:, :kernel]), filter_state[:, kernel])
    )
    step_size = jax.nn.softplus(step_raw + step_bias[None, :])
    return (inner, state_in, step_size)


def state_scan(inner, state_in, step_size, gate_z, log_decay, skip_gain, block):
    sequence_length, channels = inner.shape
    heads = step_size.shape[1]
    head = channels // heads
    state_width = state_in.shape[1] // 2
    count = sequence_length // block
    inner_blocks = inner.reshape(count, block, heads, head)
    state_input_keys = state_in[:, :state_width].reshape(count, block, state_width)
    state_output_reads = state_in[:, state_width:].reshape(count, block, state_width)
    rate = step_size * (-jnp.exp(log_decay))[None, :]
    running = jnp.cumsum(rate.reshape(count, block, heads), axis=1)
    step_blocks = step_size.reshape(count, block, heads)
    within_group = jnp.einsum(
        "xfw,xkw->xfk", state_output_reads, state_input_keys, precision=highest_precision
    )
    lower = jnp.arange(block)[:, None] >= jnp.arange(block)[None, :]
    spread = running[:, :, None, :] - running[:, None, :, :]
    decay = jnp.exp(jnp.where(lower[None, :, :, None], spread, -1e30))
    mixing = within_group[..., None] * decay * step_blocks[:, None, :, :]
    local_out = jnp.einsum("clrh,crhp->clhp", mixing, inner_blocks, precision=highest_precision)
    tail = jnp.exp(running[:, -1:, :] - running) * step_blocks
    block_state = jnp.einsum(
        "crh,crhp,crn->chpn", tail, inner_blocks, state_input_keys, precision=highest_precision
    )
    total_decay = jnp.exp(running[:, -1, :])

    carry = jnp.zeros((heads, head, state_width), inner.dtype)
    states = []
    for index in range(count):
        states.append(carry)
        carry = carry * total_decay[index][:, None, None] + block_state[index]
    entering = jnp.stack(states)
    carried = (
        jnp.einsum("cln,chpn->clhp", state_output_reads, entering, precision=highest_precision)
        * jnp.exp(running)[..., None]
    )
    result = (local_out + carried).reshape(sequence_length, channels) + inner * jnp.repeat(
        skip_gain, head
    )[None, :]
    return result * jax.nn.silu(gate_z)


def attend(query_low, keys_reduced, values_reduced, block):
    sequence_length, heads, head = query_low.shape
    scale = head ** (-0.5)
    parts = []
    totals = []
    for start in range(0, sequence_length, block):
        end = start + block
        rows = query_low[start:end]
        scores = (
            jnp.einsum("qhd,kd->hqk", rows, keys_reduced[:end], preferred_element_type=jnp.float32)
            * scale
        )
        visible = (start + jnp.arange(block))[:, None] >= jnp.arange(end)[None, :]
        scores = jnp.where(visible[None], scores, -1e30)
        peak = jnp.max(scores, axis=-1, keepdims=True)
        weights = jnp.exp(scores - peak)
        total = jnp.sum(weights, axis=-1, keepdims=True)
        shares_low = (weights / total).astype(jnp.bfloat16)
        parts.append(
            jnp.einsum(
                "hqk,kd->qhd", shares_low, values_reduced[:end], preferred_element_type=jnp.float32
            ).reshape(block, heads * head)
        )
        totals.append(peak + jnp.log(total))
    return (jnp.concatenate(parts, axis=0), totals)


def attend_back(query_low, keys_reduced, values_reduced, totals, back_mixed_low, block):
    sequence_length, heads, head = query_low.shape
    scale = head ** (-0.5)
    back_view = back_mixed_low.reshape(sequence_length, heads, head)
    back_keys = jnp.zeros((sequence_length, head), jnp.float32)
    back_values = jnp.zeros((sequence_length, head), jnp.float32)
    queries = []
    for index, start in enumerate(range(0, sequence_length, block)):
        end = start + block
        rows = query_low[start:end]
        back_rows = back_view[start:end]
        scores = (
            jnp.einsum("qhd,kd->hqk", rows, keys_reduced[:end], preferred_element_type=jnp.float32)
            * scale
        )
        visible = (start + jnp.arange(block))[:, None] >= jnp.arange(end)[None, :]
        shares = jnp.where(visible[None], jnp.exp(jnp.where(visible[None], scores - totals[index], -1e30)), 0.0)
        back_shares = jnp.einsum(
            "qhd,kd->hqk", back_rows, values_reduced[:end], preferred_element_type=jnp.float32
        )
        inner = jnp.sum(shares * back_shares, axis=-1, keepdims=True)
        back_scores = (shares * (back_shares - inner)).astype(jnp.bfloat16)
        queries.append(
            jnp.einsum(
                "hqk,kd->qhd", back_scores, keys_reduced[:end], preferred_element_type=jnp.float32
            )
            * scale
        )
        rest = ((0, sequence_length - end), (0, 0))
        back_keys = back_keys + jnp.pad(
            jnp.einsum("hqk,qhd->kd", back_scores, rows, preferred_element_type=jnp.float32)
            * scale,
            rest,
        )
        back_values = back_values + jnp.pad(
            jnp.einsum(
                "hqk,qhd->kd",
                shares.astype(jnp.bfloat16),
                back_rows,
                preferred_element_type=jnp.float32,
            ),
            rest,
        )
    return (jnp.concatenate(queries, axis=0), back_keys, back_values)


def gather_rows(values):
    return lax.all_gather(values, "tensor", axis=0, tiled=True)


def scatter_rows(values):
    return lax.psum_scatter(values, "tensor", scatter_dimension=0, tiled=True).astype(jnp.float32)


def scatter_grads(values):
    return jax.tree.map(
        lambda part: part.astype(jnp.float32),
        lax.psum_scatter(as_sent(values), "tensor", scatter_dimension=0, tiled=True),
    )


def body(
    inputs,
    cotangent,
    gain_in,
    query_weight,
    shared_matrix,
    attention_out,
    mixer_in,
    step_weight,
    filter_inner,
    filter_state,
    step_bias,
    log_decay,
    skip_gain,
    mixer_gain,
    mixer_out,
    gain_post,
    gate_up,
    down_weight,
):
    tensor_position = lax.axis_index("tensor")
    bf16 = jnp.bfloat16
    f32 = jnp.float32

    def dot(left, right):
        return jnp.dot(left, right, preferred_element_type=f32)

    def dot_t(left, right):
        return lax.dot_general(left, right, (((1,), (1,)), ((), ())), preferred_element_type=f32)

    def t_dot(left, right):
        return lax.dot_general(left, right, (((0,), (0,)), ((), ())), preferred_element_type=f32)

    own_rows = query_weight.shape[0]
    width = inputs.shape[1]
    dp_count = width // own_rows
    query_width = query_weight.shape[1]
    shared_width = shared_matrix.shape[1]
    channels = mixer_in.shape[2]
    hidden_units = gate_up.shape[2]
    step_heads = step_weight.shape[1]
    filter_rows, filter_columns = filter_state.shape
    small_width = 128

    small = jnp.concatenate(
        [
            step_weight,
            gain_in[:, None],
            gain_post[:, None],
            jnp.pad(filter_state, ((0, own_rows - filter_rows), (0, 0))),
        ],
        axis=1,
    )
    small = jnp.pad(small, ((0, 0), (0, small_width - small.shape[1])))
    first_pack = jnp.concatenate(
        [query_weight, shared_matrix, mixer_in.reshape(own_rows, 2 * channels), small], axis=1
    )
    second_pack = jnp.concatenate(
        [attention_out, mixer_out, gate_up.reshape(own_rows, 2 * hidden_units), down_weight], axis=1
    )
    seq_raw = gather_rows(inputs)
    first_all = lax.all_gather(first_pack, "dp", axis=0, tiled=True)
    first_all, second_pack, cotangent_sent = lax.optimization_barrier(
        (first_all, second_pack, cotangent)
    )
    second_all = lax.all_gather(second_pack, "dp", axis=0, tiled=True)
    back_seq = gather_rows(cotangent_sent)

    cut = query_width
    query_all = first_all[:, :cut]
    shared_all = first_all[:, cut : cut + shared_width]
    cut += shared_width
    mixer_in_all = first_all[:, cut : cut + 2 * channels]
    cut += 2 * channels
    small_all = first_all[:, cut:]
    step_all = small_all[:, :step_heads]
    gain_in_all = small_all[:, step_heads].astype(f32)
    gain_post_all = small_all[:, step_heads + 1].astype(f32)
    filter_state_all = (
        small_all[:, step_heads + 2 : step_heads + 2 + filter_columns]
        .reshape(dp_count, own_rows, filter_columns)[:, :filter_rows]
        .reshape(dp_count * filter_rows, filter_columns)
    )

    local_heads = query_width // HEAD_SIZE
    head_group = tensor_position * local_heads // (QUERY_HEADS // KEY_VALUE_HEADS)
    key_value_width = KEY_VALUE_HEADS * HEAD_SIZE
    channels_all = NH * PH
    filter_inner_f = filter_inner.astype(f32)
    step_bias_f = step_bias.astype(f32)
    log_decay_f = log_decay.astype(f32)
    skip_gain_f = skip_gain.astype(f32)
    mixer_gain_f = mixer_gain.astype(f32)
    inputs_f = inputs.astype(f32)
    scale_in = norm_scale(inputs_f)
    normed_in = inputs_f * scale_in
    seq_f = seq_raw.astype(f32)
    normed_seq = seq_f * norm_scale(seq_f)
    seq_in = (normed_seq * gain_in_all).astype(bf16)
    sequence_length = seq_in.shape[0]
    query = dot(seq_in, query_all)
    query_low = rotary_embed(
        query.reshape(sequence_length, local_heads, HEAD_SIZE), sequence_length, 1.0
    ).astype(bf16)
    key_cols = lax.dynamic_slice_in_dim(shared_all, head_group * HEAD_SIZE, HEAD_SIZE, 1)
    value_cols = lax.dynamic_slice_in_dim(
        shared_all, key_value_width + head_group * HEAD_SIZE, HEAD_SIZE, 1
    )
    used_cols = jnp.concatenate(
        [key_cols, value_cols, shared_all[:, 2 * key_value_width :]], axis=1
    )
    shared_projection = dot(seq_in, used_cols)
    keys_reduced = rotary_embed(shared_projection[:, None, :HEAD_SIZE], sequence_length, 1.0)[
        :, 0
    ].astype(bf16)
    values_reduced = shared_projection[:, HEAD_SIZE : 2 * HEAD_SIZE].astype(bf16)
    state_raw = shared_projection[:, 2 * HEAD_SIZE :]
    mixed, log_total = attend(query_low, keys_reduced, values_reduced, QB)
    mixed_low = mixed.astype(bf16)
    gate_z = dot(seq_in, mixer_in_all[:, :channels])
    inner_raw = dot(seq_in, mixer_in_all[:, channels:])
    step_raw = dot(seq_in, step_all)
    (inner, state_in, step_size), mixer_back = jax.vjp(
        mixer_input,
        inner_raw,
        state_raw,
        step_raw,
        filter_inner_f,
        filter_state_all.astype(f32),
        step_bias_f,
    )
    inner_low = inner.astype(bf16)
    state_low = state_in.astype(bf16)

    def scan_piece(inner_v, state_v, step_v, gate_v, decay_v, skip_v):
        return state_scan(inner_v, state_v, step_v, gate_v, decay_v, skip_v, BLK)

    gated, scan_back = jax.vjp(
        scan_piece,
        inner_low.astype(f32),
        state_low.astype(f32),
        step_size,
        gate_z,
        log_decay_f,
        skip_gain_f,
    )
    total_squares = lax.psum(jnp.sum(gated * gated, axis=1), "tensor")
    gated_scale = lax.rsqrt(total_squares / channels_all + epsilon)[:, None]
    gated_norm = gated * gated_scale
    mixer_low = (gated_norm * mixer_gain_f).astype(bf16)

    cut = query_width
    attention_all = second_all[:, :cut]
    mixer_out_all = second_all[:, cut : cut + channels]
    cut += channels
    gate_up_all = second_all[:, cut : cut + 2 * hidden_units]
    cut += 2 * hidden_units
    down_all = second_all[:, cut:]

    branch_low = (dot_t(mixed_low, attention_all) + dot_t(mixer_low, mixer_out_all)).astype(bf16)
    hidden = inputs_f + scatter_rows(branch_low)
    scale_post = norm_scale(hidden)
    normed_post = hidden * scale_post
    rows_post_low = (normed_post * gain_post_all).astype(bf16)
    seq_post = gather_rows(rows_post_low)
    gate = dot(seq_post, gate_up_all[:, :hidden_units])
    upper = dot(seq_post, gate_up_all[:, hidden_units:])
    sigmoid_gate = jax.nn.sigmoid(gate)
    silu_gate = gate * sigmoid_gate
    activated_low = (silu_gate * upper).astype(bf16)
    down_low = dot_t(activated_low, down_all).astype(bf16)

    back_act = dot(back_seq, down_all)
    back_gate = back_act * upper * sigmoid_gate * (1.0 + gate * (1.0 - sigmoid_gate))
    back_upper = back_act * silu_gate
    back_gu_low = jnp.concatenate([back_gate, back_upper], axis=1).astype(bf16)
    back_post_low = dot_t(back_gu_low, gate_up_all).astype(bf16)
    back_post = scatter_rows(back_post_low)
    back_down_w = t_dot(back_seq, activated_low).astype(bf16)
    back_gate_up_w = t_dot(seq_post, back_gu_low).astype(bf16)
    back_gain_post = jnp.sum(back_post * normed_post, axis=0)
    back_norm_post = back_post * gain_post_all
    back_hidden = cotangent.astype(f32) + scale_post * (
        back_norm_post - normed_post * jnp.mean(back_norm_post * normed_post, axis=1, keepdims=True)
    )
    back_mix = gather_rows(back_hidden.astype(bf16))
    output = (hidden + scatter_rows(down_low)).astype(bf16)

    back_mixer_out_w = t_dot(back_mix, mixer_low).astype(bf16)
    back_attention_w = t_dot(back_mix, mixed_low).astype(bf16)
    early = jnp.concatenate(
        [back_attention_w, back_mixer_out_w, back_gate_up_w, back_down_w], axis=1
    )
    early, back_mix = lax.optimization_barrier((early, back_mix))
    early_rows = lax.psum_scatter(early, "dp", scatter_dimension=0, tiled=True)

    back_norm = dot(back_mix, mixer_out_all)
    back_mixer_gain = jnp.sum(back_norm * gated_norm, axis=0)
    back_scaled = back_norm * mixer_gain_f
    inner_total = lax.psum(jnp.sum(back_scaled * gated_norm, axis=1), "tensor")
    back_gated = gated_scale * (back_scaled - gated_norm * (inner_total / channels_all)[:, None])
    back_inner, back_state, back_step_size, back_gate_z, back_log_decay, back_skip_gain = scan_back(
        back_gated
    )
    (
        back_inner_raw,
        back_state_raw,
        back_step_raw,
        back_filter_inner,
        back_filter_state,
        back_step_bias,
    ) = mixer_back((back_inner, back_state, back_step_size))
    back_mixer_low = jnp.concatenate([back_gate_z, back_inner_raw], axis=1).astype(bf16)
    back_step_low = back_step_raw.astype(bf16)
    back_mixed_low = dot(back_mix, attention_all).astype(bf16)
    back_query_rot, back_keys_rot, back_values = attend_back(
        query_low, keys_reduced, values_reduced, log_total, back_mixed_low, QB
    )
    back_query_low = (
        rotary_embed(back_query_rot, sequence_length, -1.0)
        .reshape(sequence_length, local_heads * HEAD_SIZE)
        .astype(bf16)
    )
    back_keys = rotary_embed(back_keys_rot[:, None, :], sequence_length, -1.0)[:, 0]
    back_used_low = jnp.concatenate([back_keys, back_values, back_state_raw], axis=1).astype(bf16)
    used_width = back_used_low.shape[1]

    back_in_part = (
        dot_t(back_query_low, query_all)
        + dot_t(back_mixer_low, mixer_in_all)
        + dot_t(back_step_low, step_all)
        + dot_t(back_used_low, used_cols)
    )
    back_gain_in = jnp.sum(back_in_part * normed_seq, axis=0)
    back_in_rows = scatter_rows(back_in_part.astype(bf16))

    spread_state = jnp.pad(
        back_filter_state.reshape(dp_count, filter_rows, filter_columns),
        ((0, 0), (0, own_rows - filter_rows), (0, 0)),
    ).reshape(width, filter_columns)
    back_small = jnp.concatenate(
        [
            t_dot(seq_in, back_step_low),
            back_gain_in[:, None],
            back_gain_post[:, None],
            spread_state,
        ],
        axis=1,
    )
    back_small = jnp.pad(back_small, ((0, 0), (0, small_width - back_small.shape[1])))
    late = jnp.concatenate(
        [
            t_dot(seq_in, back_query_low).astype(bf16),
            t_dot(seq_in, back_used_low).astype(bf16),
            t_dot(seq_in, back_mixer_low).astype(bf16),
            back_small.astype(bf16),
        ],
        axis=1,
    )
    late_rows = lax.psum_scatter(late, "dp", scatter_dimension=0, tiled=True)

    cut = query_width
    back_query_w = late_rows[:, :cut].astype(f32)
    used_rows = late_rows[:, cut : cut + used_width]
    cut += used_width
    back_mixer_in_w = late_rows[:, cut : cut + 2 * channels].astype(f32)
    cut += 2 * channels
    small_rows = late_rows[:, cut:]
    back_step_w = small_rows[:, :step_heads].astype(f32)
    select_heads = (jnp.arange(KEY_VALUE_HEADS) == head_group).astype(bf16)
    pair = (
        used_rows[:, : 2 * HEAD_SIZE].reshape(own_rows, 2, 1, HEAD_SIZE)
        * select_heads[None, None, :, None]
    ).reshape(own_rows, 2 * key_value_width)
    common = lax.psum(
        jnp.concatenate([pair, used_rows[:, 2 * HEAD_SIZE :], small_rows], axis=1), "tensor"
    ).astype(f32)
    back_shared_w = common[:, :shared_width]
    common = common[:, shared_width:]
    back_gain_in = common[:, step_heads]
    back_gain_post = common[:, step_heads + 1]
    back_filter_state = common[:filter_rows, step_heads + 2 : step_heads + 2 + filter_columns]

    cut = query_width
    back_attention_w = early_rows[:, :cut].astype(f32)
    back_mixer_out_w = early_rows[:, cut : cut + channels].astype(f32)
    cut += channels
    back_gate_up_w = early_rows[:, cut : cut + 2 * hidden_units].astype(f32)
    cut += 2 * hidden_units
    back_down_w = early_rows[:, cut:].astype(f32)

    back_norm_in = back_in_rows * gain_in_all
    back_inputs = back_hidden + scale_in * (
        back_norm_in - normed_in * jnp.mean(back_norm_in * normed_in, axis=1, keepdims=True)
    )
    pieces = (back_filter_inner, back_step_bias, back_log_decay, back_skip_gain, back_mixer_gain)
    flat = jnp.concatenate([piece.reshape(-1) for piece in pieces])
    flat = jnp.pad(flat, (0, -flat.shape[0] % 1024))
    flat = lax.psum(flat, "dp")
    results = []
    cut = 0
    for piece in pieces:
        results.append(flat[cut : cut + piece.size].reshape(piece.shape))
        cut += piece.size
    back_filter_inner, back_step_bias, back_log_decay, back_skip_gain, back_mixer_gain = results
    return (
        output,
        back_inputs,
        back_gain_in,
        back_query_w,
        back_shared_w,
        back_attention_w,
        back_mixer_in_w.reshape(own_rows, 2, channels),
        back_step_w,
        back_filter_inner,
        back_filter_state,
        back_step_bias,
        back_log_decay,
        back_skip_gain,
        back_mixer_gain,
        back_mixer_out_w,
        back_gain_post,
        back_gate_up_w.reshape(own_rows, 2, hidden_units),
        back_down_w,
    )


def solution(mesh):
    in_specs = (
        P(("dp", "tensor"), None),
        P(("dp", "tensor"), None),
        P("dp"),
        P("dp", "tensor"),
        P("dp", None),
        P("dp", "tensor"),
        P("dp", None, "tensor"),
        P("dp", "tensor"),
        P(None, "tensor"),
        P("dp", None),
        P("tensor"),
        P("tensor"),
        P("tensor"),
        P("tensor"),
        P("dp", "tensor"),
        P("dp"),
        P("dp", None, "tensor"),
        P("dp", "tensor"),
    )
    out_specs = (
        P(("dp", "tensor"), None),
        P(("dp", "tensor"), None),
        P("dp"),
        P("dp", "tensor"),
        P("dp", None),
        P("dp", "tensor"),
        P("dp", None, "tensor"),
        P("dp", "tensor"),
        P(None, "tensor"),
        P("dp", None),
        P("tensor"),
        P("tensor"),
        P("tensor"),
        P("tensor"),
        P("dp", "tensor"),
        P("dp"),
        P("dp", None, "tensor"),
        P("dp", "tensor"),
    )
    return jax.shard_map(body, mesh=mesh, in_specs=in_specs, out_specs=out_specs, check_vma=False)
```

time: 1380 us -> 810 us (0.59)
  waiting for transfers between devices: 751 us -> 419 us
  blocking collectives: 265 us -> 48.9 us
    reduce_scatter x9 -> x0, waiting for transfers between devices: 452 us -> none  [the longest x1 68.4 us: body(): lax.psum_scatter(back_gate_up_w.astype(jnp.bfloat16), 'dp', scatter_dimen...]
    all_gather x7 -> x0, blocking collectives: 191 us -> none  [the longest x1 33.9 us: body(): lax.all_gather(mixer_out, 'dp', axis=0, tiled=True)]
    unnamed x26 -> x15, waiting for transfers between devices: 104 us -> 157 us
    reduce_scatter x2 -> x4, waiting for transfers between devices: 42.7 us -> 78.8 us  [scatter_rows(): lax.psum_scatter(values, 'tensor', scatter_dimension=0, tiled=True)]
    psum x1, waiting for transfers between devices: 1.58 us -> 28.6 us  [body(): lax.psum(jnp.concatenate([pair, used_rows[:, 2 * HEAD_SIZE:], small_rows]...]
    unnamed x1 -> x0, blocking collectives: 21.4 us -> none
    dynamic_update_slice x20 -> x0, local copies, waits for them, and re-layouts: 16.5 us -> none  [the longest x4 12 us: attend(): mixed, log_total = lax.map(one_block, jnp.arange(count))]
    unnamed x321 -> x372, local copies, waits for them, and re-layouts: 36.3 us -> 46.4 us
  transfers between devices with their start and end apart: 23 -> 13, of which waited for: 19 -> 12; matrix products, arithmetic and copies ran while one was open for 9% -> 12% of each run, Pallas kernels for 0% -> 0%
where the time goes in v1:
time: 810 us; the launch traced here: 800 us
  waiting for transfers between devices  419 us (52%)
  matrix products  123 us (15%)
  local copies, waits for them, and re-layouts  100 us (12%)
  other arithmetic  91.4 us (11%)
  blocking collectives  48.9 us (6%)
  between operations  16.2 us (2%)
    unnamed x15, waiting for transfers between devices  157 us
    reduce_scatter x4, waiting for transfers between devices, scatter_rows(): lax.psum_scatter(values, 'tensor', scatter_dimension=0, tiled=True)  78.8 us
    all_gather x4, waiting for transfers between devices, gather_rows(): return lax.all_gather(values, 'tensor', axis=0, tiled=True)  63.9 us
    all_gather x1, waiting for transfers between devices, body(): first_all = lax.all_gather(first_pack, 'dp', axis=0, tiled=True)  63.6 us
    unnamed x372, local copies, waits for them, and re-layouts  46.4 us
    psum x1, blocking collectives, body(): flat = lax.psum(flat, 'dp')  35.3 us
    dot_general x10, matrix products, dot(): return jnp.dot(left, right, preferred_element_type=f32)  34.3 us
    psum x1, waiting for transfers between devices, body(): lax.psum(jnp.concatenate([pair, used_rows[:, 2 * HEAD_SIZE:], small_rows]...  28.6 us
  transfers between devices with their start and end apart: 13, of which 12 were waited for; matrix products, arithmetic and copies ran while one was open for 12% of the time, Pallas kernels for 0%

profile of v1, /device:TPU:0, one launch (start us, length us, event | category | flops | bytes accessed | tf_op | source)
XLA Modules:
  0.0 800.3 jit_solution(3163510258269708298)
XLA Ops:
  19.4 15.7 %all-gather.7.cloned.1.call-done = bf16[1024,1024]{1,0:T(8,128)(2,1)} async-done(((bf16[256,1024]{1,0:T(8,128)(2,1)}), bf16[1024,1024]{1,0:T(8,128)(2,1)}) %all-gather.7.cloned.1.call-update) | async-done | bytes 2097168 | tf_op jit(solution)/shard_map/all_gather | solution.py:182
  37.1 63.6 %all-gather.9.cloned.1.call-done = bf16[1024,1536]{0,1:T(8,128)(2,1)} async-done(((bf16[128,1536]{0,1:T(8,128)(2,1)}), bf16[1024,1536]{0,1:T(8,128)(2,1)}) %all-gather.9.cloned.1.call-update) | async-done | bytes 3145744 | tf_op jit(solution)/shard_map/all_gather | solution.py:257
  102.6 2.3 slice.318
  107.6 2.1 fusion.2
  109.8 3.6 fusion.125
  121.2 3.3 fusion.247
  128.0 2.2 fusion.241
  132.1 5.7 multiply_convert_fusion.4
  137.9 2.3 copy.261
  140.2 2.2 copy.354
  144.5 4.3 multiply_convert_fusion.6
  149.0 2.3 fusion.51
  154.4 3.5 bitcast_add_fusion.1
  160.3 3.1 copy.272
  165.3 5.6 multiply_reduce_fusion.9
  170.9 7.0 psum.28
  187.5 2.2 fusion.94
  189.7 26.3 %all-gather.11.cloned.1.call-done = bf16[1024,2048]{1,0:T(8,128)(2,1)} async-done(((bf16[128,2048]{1,0:T(8,128)(2,1)}), bf16[1024,2048]{1,0:T(8,128)(2,1)}) %all-gather.11.cloned.1.call-update) | async-done | bytes 4194320 | tf_op jit(solution)/shard_map/all_gather | solution.py:261
  217.9 3.9 add_convert_fusion
  222.5 29.2 %reduce-scatter.11.cloned.1.call-done = bf16[256,1024]{1,0:T(8,128)(2,1)} async-done(((bf16[1024,1024]{1,0:T(8,128)(2,1)}), bf16[256,1024]{1,0:T(8,128)(2,1)}) %reduce-scatter.11.cloned.1.call-update) | async-done | bytes 524304 | tf_op jit(solution)/shard_map/reduce_scatter | solution.py:186
  255.9 19.9 %all-gather.15.cloned.1.call-done = bf16[1024,1024]{1,0:T(8,128)(2,1)} async-done(((bf16[256,1024]{1,0:T(8,128)(2,1)}), bf16[1024,1024]{1,0:T(8,128)(2,1)}) %all-gather.15.cloned.1.call-update) | async-done | bytes 2097168 | tf_op jit(solution)/shard_map/all_gather | solution.py:182
  275.8 4.4 fusion.115
  280.2 19.7 %all-gather.13.cloned.1.call-done = bf16[1024,1024]{1,0:T(8,128)(2,1)} async-done(((bf16[256,1024]{1,0:T(8,128)(2,1)}), bf16[1024,1024]{1,0:T(8,128)(2,1)}) %all-gather.13.cloned.1.call-update) | async-done | bytes 2097168 | tf_op jit(solution)/shard_map/all_gather | solution.py:182
  299.9 3.3 fusion.108
  303.7 4.8 multiply_convert_fusion.1
  309.8 3.7 fusion.33
  313.6 31.5 %reduce-scatter.15.cloned.1.call-done = bf16[256,1024]{1,0:T(8,128)(2,1)} async-done(((bf16[1024,1024]{1,0:T(8,128)(2,1)}), bf16[256,1024]{1,0:T(8,128)(2,1)}) %reduce-scatter.15.cloned.1.call-update) | async-done | bytes 524304 | tf_op jit(solution)/shard_map/reduce_scatter | solution.py:186
  345.1 2.4 fusion.103
  348.1 2.6 fusion.233
  353.8 2.1 bitcast_add_fusion.10
  355.9 4.5 convolution_convert_fusion.3
  360.4 3.7 convolution_convert_fusion
  364.7 8.7 %all-gather.17.cloned.1.call-done = bf16[1024,1024]{1,0:T(8,128)(2,1)} async-done(((bf16[256,1024]{1,0:T(8,128)(2,1)}), bf16[1024,1024]{1,0:T(8,128)(2,1)}) %all-gather.17.cloned.1.call-update) | async-done | bytes 2097168 | tf_op jit(solution)/shard_map/all_gather | solution.py:182
  373.4 3.3 convolution_convert_fusion.5
  378.4 2.3 pad_maximum_fusion
  380.7 4.2 multiply_reduce_fusion.2
  384.9 6.6 psum.29
  392.2 5.5 fusion.40
  397.7 3.0 copy.277
  403.8 3.6 fusion.81
  414.5 3.5 fusion.77
  423.9 6.0 fusion.37
  431.4 4.7 bitcast_add_fusion
  443.2 2.7 fusion.170
  449.4 2.4 fusion.239
  458.6 3.4 fusion.189
  465.8 3.1 copy.281
  469.0 6.1 multiply_reduce_fusion.6
  477.6 3.8 fusion.47
  481.4 3.0 convolution_convert_fusion.2
  484.4 2.7 fusion.5
  489.6 2.8 fusion.162
  496.6 2.1 broadcast_multiply_fusion.4
  503.2 2.7 fusion.107
  508.9 4.9 fusion.3
  515.7 4.6 copy.338
  521.5 3.9 convolution_convert_fusion.1
  525.6 67.8 %reduce-scatter.19.cloned.1.call-done = bf16[128,1408]{1,0:T(8,128)(2,1)} async-done(((bf16[1024,1408]{1,0:T(8,128)(2,1)}), bf16[128,1408]{1,0:T(8,128)(2,1)}) %reduce-scatter.19.cloned.1.call-update) | async-done | bytes 360464
  596.3 6.5 copy.340
  603.9 35.3 %psum.31 = f32[3072]{0:T(1024)S(1)} all-reduce(f32[3072]{0:T(1024)S(1)} %pad.209), channel_id=1, replica_groups=mesh['dp'=8,'tensor'=4] {'dp'}, use_global_device_ids=true, to_apply=%region_54.55 | all-reduce | flops 3072 | bytes 24576 | tf_op jit(solution)/shard_map/psum | solution.py:494
  642.5 18.1 %reduce-scatter.13.cloned.1.call-done = bf16[256,1024]{1,0:T(8,128)(2,1)} async-done(((bf16[1024,1024]{1,0:T(8,128)(2,1)}), bf16[256,1024]{1,0:T(8,128)(2,1)}) %reduce-scatter.13.cloned.1.call-update) | async-done | bytes 524304 | tf_op jit(solution)/shard_map/reduce_scatter | solution.py:186
  660.6 3.1 fusion.99
  666.3 28.6 %all-reduce.49.cloned.1.call-done = bf16[128,640]{0,1:T(8,128)(2,1)} async-done(((bf16[128,640]{0,1:T(8,128)(2,1)}), bf16[128,640]{0,1:T(8,128)(2,1)}) %all-reduce.49.cloned.1.call-update) | async-done | bytes 163856 | tf_op jit(solution)/shard_map/psum | solution.py:470
  699.3 87.7 %reduce-scatter.21.cloned.1.call-done = bf16[128,2048]{1,0:T(8,128)(2,1)} async-done(((bf16[1024,2048]{1,0:T(8,128)(2,1)}), bf16[128,2048]{1,0:T(8,128)(2,1)}) %reduce-scatter.21.cloned.1.call-update) | async-done | bytes 524304
  (555 shorter events, 144.6 us)
Async XLA Ops:
  7.2 5.5 copy-start.76
  7.2 5.6 copy-start.160
  7.2 5.6 copy-start.146
  7.2 5.6 copy-start.157
  7.2 6.3 copy-start.155
  7.2 9.6 %copy-start.161 = (bf16[6]{0:T(256)(128)(2,1)S(1)}, bf16[6]{0:T(256)(128)(2,1)}, u32[]{:S(2)}) copy-start(bf16[6]{0:T(256)(128)(2,1)} %param.29) | copy-start | bytes 40
  7.3 10.9 %copy-start.78 = (bf16[128,512]{1,0:T(8,128)(2,1)S(1)}, bf16[128,512]{1,0:T(8,128)(2,1)}, u32[]{:S(2)}) copy-start(bf16[128,512]{1,0:T(8,128)(2,1)} %param.35) | copy-start | bytes 393220
  7.3 10.8 %copy-start.81 = (bf16[128,384]{1,0:T(8,128)(2,1)S(1)}, bf16[128,384]{1,0:T(8,128)(2,1)}, u32[]{:S(2)}) copy-start(bf16[128,384]{1,0:T(8,128)(2,1)} %param.32) | copy-start | bytes 294916
  7.3 10.8 %copy-start.85 = (bf16[128,128]{1,0:T(8,128)(2,1)S(1)}, bf16[128,128]{1,0:T(8,128)(2,1)}, u32[]{:S(2)}) copy-start(bf16[128,128]{1,0:T(8,128)(2,1)} %param.23) | copy-start | bytes 98308
  7.3 27.7 %all-gather.7.cloned.1.call-start = ((), (), s32[]{:S(2)}) async-start(), calls=%async_computation.6 | async-start | bytes 2621440 | tf_op jit(solution)/shard_map/all_gather | solution.py:182
  8.0 92.7 %all-gather.9.cloned.1.call-start = ((), (), s32[]{:S(2)}) async-start(), calls=%async_computation.7 | async-start | bytes 3538944 | tf_op jit(solution)/shard_map/all_gather | solution.py:257
  12.6 203.4 %all-gather.11.cloned.1.call-start = ((), (), s32[]{:S(2)}) async-start(), calls=%async_computation.8 | async-start | bytes 4718592 | tf_op jit(solution)/shard_map/all_gather | solution.py:261
  14.1 23.0 %copy-start.147 = (f32[32]{0:T(128)}, f32[32]{0:T(128)S(1)}, u32[]{:S(2)}) copy-start(f32[32]{0:T(128)S(1)} %multiply_power_fusion) | copy-start | bytes 388
  16.9 97.9 %copy-start.151 = (f32[6]{0:T(128)}, f32[6]{0:T(128)S(1)}, u32[]{:S(2)}) copy-start(f32[6]{0:T(128)S(1)} %fusion.196) | copy-start | bytes 76
  19.3 168.2 %copy-start.23 = (pred[512,1024]{0,1:T(8,128)(4,1)}, pred[512,1024]{0,1:T(8,128)(4,1)S(1)}, u32[]{:S(2)}) copy-start(pred[512,1024]{0,1:T(8,128)(4,1)S(1)} %iota_compare_fusion) | copy-start | bytes 1572868
  105.7 4.1 copy-start.83
  126.1 6.0 copy-start.94
  126.1 6.0 copy-start.96
  126.1 6.0 copy-start.98
  126.1 6.0 copy-start.100
  126.1 6.0 copy-start.134
  127.0 17.5 %copy-start.124 = (f32[1,256]{1,0:T(1,128)}, f32[1,256]{1,0:T(1,128)S(1)}, u32[]{:S(2)}) copy-start(f32[1,256]{1,0:T(1,128)S(1)} %get-tuple-element.232) | copy-start | bytes 3076
  127.0 17.5 %copy-start.126 = (f32[1,256]{1,0:T(1,128)}, f32[1,256]{1,0:T(1,128)S(1)}, u32[]{:S(2)}) copy-start(f32[1,256]{1,0:T(1,128)S(1)} %get-tuple-element.233) | copy-start | bytes 3076
  127.0 17.5 %copy-start.128 = (f32[1,256]{1,0:T(1,128)}, f32[1,256]{1,0:T(1,128)S(1)}, u32[]{:S(2)}) copy-start(f32[1,256]{1,0:T(1,128)S(1)} %get-tuple-element.234) | copy-start | bytes 3076
  127.0 17.5 %copy-start.130 = (f32[1,256]{1,0:T(1,128)}, f32[1,256]{1,0:T(1,128)S(1)}, u32[]{:S(2)}) copy-start(f32[1,256]{1,0:T(1,128)S(1)} %get-tuple-element.235) | copy-start | bytes 3076
  137.9 6.6 copy-start.149
  142.4 6.5 copy-start.116
  144.3 107.4 %reduce-scatter.11.cloned.1.call-start = ((), (), s32[]{:S(2)}) async-start(), calls=%async_computation.9 | async-start | bytes 2621440 | tf_op jit(solution)/shard_map/reduce_scatter | solution.py:186
  153.0 4.9 copy-start.67
  153.9 4.0 copy-start.19
  160.3 5.0 copy-start.104
  177.9 4.2 copy-start.70
  221.8 29.9 %copy-start = (bf16[256,1024]{1,0:T(8,128)(2,1)S(1)}, bf16[256,1024]{1,0:T(8,128)(2,1)}, u32[]{:S(2)}) copy-start(bf16[256,1024]{1,0:T(8,128)(2,1)} %param.18) | copy-start | bytes 1572868
  221.8 54.0 %all-gather.15.cloned.1.call-start = ((), (), s32[]{:S(2)}) async-start(), calls=%async_computation.12 | async-start | bytes 2621440 | tf_op jit(solution)/shard_map/all_gather | solution.py:182
  222.4 77.5 %all-gather.13.cloned.1.call-start = ((), (), s32[]{:S(2)}) async-start(), calls=%async_computation.10 | async-start | bytes 2621440 | tf_op jit(solution)/shard_map/all_gather | solution.py:182
  255.6 89.5 %reduce-scatter.15.cloned.1.call-start = ((), (), s32[]{:S(2)}) async-start(), calls=%async_computation.13 | async-start | bytes 2621440 | tf_op jit(solution)/shard_map/reduce_scatter | solution.py:186
  313.5 59.9 %all-gather.17.cloned.1.call-start = ((), (), s32[]{:S(2)}) async-start(), calls=%async_computation.14 | async-start | bytes 2621440 | tf_op jit(solution)/shard_map/all_gather | solution.py:182
  350.7 242.7 %reduce-scatter.19.cloned.1.call-start = ((), (), s32[]{:S(2)}) async-start(), calls=%async_computation.17 | async-start | bytes 3244032
  355.9 4.5 copy-start.159
  355.9 4.5 copy-start.167
  355.9 4.5 copy-start.169
  403.8 9.5 %copy-start.8 = (f32[8,6,64,128]{3,2,1,0:T(8,128)}, f32[8,6,64,128]{3,2,1,0:T(8,128)S(1)}, u32[]{:S(2)}) copy-start(f32[8,6,64,128]{3,2,1,0:T(8,128)S(1)} %fusion.72) | copy-start | bytes 4718596
  469.0 6.1 copy-start.95
  469.0 6.1 copy-start.97
  469.0 6.1 copy-start.99
  469.0 6.1 copy-start.101
  503.1 3.8 copy-start.5
  503.2 3.8 copy-start.61
  508.9 5.0 copy-start.82
  508.9 5.0 copy-start.111
  508.9 5.0 copy-start.43
  520.3 120.8 %reduce-scatter.17.cloned.1.call-start = ((), (), s32[]{:S(2)}) async-start(), calls=%async_computation.15 | async-start | bytes 2621440 | tf_op jit(solution)/shard_map/reduce_scatter | solution.py:186
  520.9 139.7 %reduce-scatter.13.cloned.1.call-start = ((), (), s32[]{:S(2)}) async-start(), calls=%async_computation.11 | async-start | bytes 2621440 | tf_op jit(solution)/shard_map/reduce_scatter | solution.py:186
  525.4 169.5 %all-reduce.49.cloned.1.call-start = ((), (), s32[]{:S(2)}) async-start(), calls=%async_computation.16 | async-start | bytes 327680 | tf_op jit(solution)/shard_map/psum | solution.py:470
  596.2 190.8 %reduce-scatter.21.cloned.1.call-start = ((), (), s32[]{:S(2)}) async-start(), calls=%async_computation.18 | async-start | bytes 4718592
  602.8 38.2 %copy-start.84 = (f32[1024,1]{0,1:T(1,128)S(1)}, f32[1024,1]{0,1:T(1,128)}, u32[]{:S(2)}) copy-start(f32[1024,1]{0,1:T(1,128)} %copy-done.83) | copy-start | bytes 12292
  602.8 57.7 %copy-start.7 = (bf16[256,1024]{1,0:T(8,128)(2,1)S(1)}, bf16[256,1024]{1,0:T(8,128)(2,1)}, u32[]{:S(2)}) copy-start(bf16[256,1024]{1,0:T(8,128)(2,1)} %reduce-scatter.11.cloned.1.call-done) | copy-start | bytes 1572868
  602.9 57.7 %copy-start.25 = (bf16[256,1024]{1,0:T(8,128)(2,1)S(1)}, bf16[256,1024]{1,0:T(8,128)(2,1)}, u32[]{:S(2)}) copy-start(bf16[256,1024]{1,0:T(8,128)(2,1)} %param.19) | copy-start | bytes 1572868
  602.9 57.7 %copy-start.26 = (bf16[256,1024]{1,0:T(8,128)(2,1)S(1)}, bf16[256,1024]{1,0:T(8,128)(2,1)}, u32[]{:S(2)}) copy-start(bf16[256,1024]{1,0:T(8,128)(2,1)} %reduce-scatter.15.cloned.1.call-done) | copy-start | bytes 1572868
  602.9 57.7 %copy-start.91 = (f32[256]{0:T(256)S(1)}, f32[256]{0:T(256)}, u32[]{:S(2)}) copy-start(f32[256]{0:T(256)} %copy-done.90) | copy-start | bytes 3076
  602.9 57.7 %copy-start.133 = (f32[256]{0:T(256)S(1)}, f32[256]{0:T(256)}, u32[]{:S(2)}) copy-start(f32[256]{0:T(256)} %copy-done.132) | copy-start | bytes 3076
  642.4 22.1 %slice-start = ((bf16[128,1408]{1,0:T(8,128)(2,1)}), bf16[128,768]{1,0:T(8,128)(2,1)S(1)}, s32[]{:S(2)}) async-start(bf16[128,1408]{1,0:T(8,128)(2,1)} %reduce-scatter.19.cloned.1.call-done), calls=%async_computation.19 | async-start | bytes 393216 | tf_op jit(solution)/shard_map/slice | solution.py:461
  642.5 23.2 %slice-start.1 = ((bf16[128,1408]{1,0:T(8,128)(2,1)}), bf16[128,6]{1,0:T(8,128)(2,1)S(1)}, s32[]{:S(2)}) async-start(bf16[128,1408]{1,0:T(8,128)(2,1)} %reduce-scatter.19.cloned.1.call-done), calls=%async_computation.20 | async-start | bytes 65536 | tf_op jit(solution)/shard_map/slice | solution.py:464
  787.0 5.6 slice-start.2
  (122 other events, 250.9 us)
Sparse Core Ops, SparseCore 0:
  9.7 25.2 all-gather.6
  37.6 63.0 all-gather.8
  144.4 71.5 all-gather.10
  222.0 29.7 reduce-scatter.10
  253.2 22.5 all-gather.14
  277.3 22.5 all-gather.12
  313.6 31.3 reduce-scatter.14
  350.8 22.5 all-gather.16
  520.4 72.9 reduce-scatter.18
  595.7 30.5 reduce-scatter.16
  629.1 31.4 reduce-scatter.12
  663.3 31.5 all-reduce.48
  699.0 88.0 reduce-scatter.20

commit v2 on v1

--- a/solution.py
+++ b/solution.py
@@ -178,19 +178,57 @@
     return (jnp.concatenate(queries, axis=0), back_keys, back_values)
 
 
+def swap(values, axis, count, bit):
+    return lax.ppermute(values, axis, [(i, i ^ bit) for i in range(count)])
+
+
 def gather_rows(values):
-    return lax.all_gather(values, "tensor", axis=0, tiled=True)
+    count = lax.axis_size("tensor")
+    if count & (count - 1):
+        return lax.all_gather(values, "tensor", axis=0, tiled=True)
+    index = lax.axis_index("tensor")
+    rows, width = values.shape
+    held = values[None]
+    bit = count // 2
+    while bit:
+        other = swap(held, "tensor", count, bit)
+        low = (index // bit) % 2 == 0
+        held = jnp.stack([jnp.where(low, held, other), jnp.where(low, other, held)], axis=1)
+        held = held.reshape(-1, rows, width)
+        bit //= 2
+    return held.reshape(count * rows, width)
 
 
 def scatter_rows(values):
-    return lax.psum_scatter(values, "tensor", scatter_dimension=0, tiled=True).astype(jnp.float32)
-
-
-def scatter_grads(values):
-    return jax.tree.map(
-        lambda part: part.astype(jnp.float32),
-        lax.psum_scatter(as_sent(values), "tensor", scatter_dimension=0, tiled=True),
-    )
+    count = lax.axis_size("tensor")
+    if count & (count - 1):
+        return lax.psum_scatter(values, "tensor", scatter_dimension=0, tiled=True).astype(
+            jnp.float32
+        )
+    index = lax.axis_index("tensor")
+    rows = values.shape[0] // count
+    width = values.shape[1]
+    total = values.reshape(count, rows, width)
+    bit = 1
+    while bit < count:
+        pairs = total.reshape(-1, 2, rows, width)
+        mine = (index // bit) % 2
+        kept = lax.dynamic_index_in_dim(pairs, mine, 1, keepdims=False)
+        sent = lax.dynamic_index_in_dim(pairs, 1 - mine, 1, keepdims=False).astype(jnp.bfloat16)
+        total = kept.astype(jnp.float32) + swap(sent, "tensor", count, bit).astype(jnp.float32)
+        bit *= 2
+    return total.reshape(rows, width)
+
+
+def sum_all(values, axis):
+    count = lax.axis_size(axis)
+    if count & (count - 1):
+        return lax.psum(values, axis)
+    bit = 1
+    while bit < count:
+        values = values + swap(values, axis, count, bit)
+        bit *= 2
+    return values
 
 
 def body(
@@ -352,6 +390,7 @@
     cut += 2 * hidden_units
     down_all = second_all[:, cut:]
 
+    mixer_low, back_seq = lax.optimization_barrier((mixer_low, back_seq))
     branch_low = (dot_t(mixed_low, attention_all) + dot_t(mixer_low, mixer_out_all)).astype(bf16)
     hidden = inputs_f + scatter_rows(branch_low)
     scale_post = norm_scale(hidden)
@@ -379,14 +418,14 @@
         back_norm_post - normed_post * jnp.mean(back_norm_post * normed_post, axis=1, keepdims=True)
     )
     back_mix = gather_rows(back_hidden.astype(bf16))
-    output = (hidden + scatter_rows(down_low)).astype(bf16)
 
     back_mixer_out_w = t_dot(back_mix, mixer_low).astype(bf16)
     back_attention_w = t_dot(back_mix, mixed_low).astype(bf16)
     early = jnp.concatenate(
         [back_attention_w, back_mixer_out_w, back_gate_up_w, back_down_w], axis=1
     )
-    early, back_mix = lax.optimization_barrier((early, back_mix))
+    early, back_mix, down_low = lax.optimization_barrier((early, back_mix, down_low))
+    down_rows = scatter_rows(down_low)
     early_rows = lax.psum_scatter(early, "dp", scatter_dimension=0, tiled=True)
 
     back_norm = dot(back_mix, mixer_out_all)
@@ -420,6 +459,10 @@
     back_used_low = jnp.concatenate([back_keys, back_values, back_state_raw], axis=1).astype(bf16)
     used_width = back_used_low.shape[1]
 
+    back_mixer_low, back_query_low, back_used_low, early_rows, down_rows = lax.optimization_barrier(
+        (back_mixer_low, back_query_low, back_used_low, early_rows, down_rows)
+    )
+    output = (hidden + down_rows).astype(bf16)
     back_in_part = (
         dot_t(back_query_low, query_all)
         + dot_t(back_mixer_low, mixer_in_all)
@@ -467,7 +510,7 @@
         used_rows[:, : 2 * HEAD_SIZE].reshape(own_rows, 2, 1, HEAD_SIZE)
         * select_heads[None, None, :, None]
     ).reshape(own_rows, 2 * key_value_width)
-    common = lax.psum(
+    common = sum_all(
         jnp.concatenate([pair, used_rows[:, 2 * HEAD_SIZE :], small_rows], axis=1), "tensor"
     ).astype(f32)
     back_shared_w = common[:, :shared_width]
@@ -491,7 +534,7 @@
     pieces = (back_filter_inner, back_step_bias, back_log_decay, back_skip_gain, back_mixer_gain)
     flat = jnp.concatenate([piece.reshape(-1) for piece in pieces])
     flat = jnp.pad(flat, (0, -flat.shape[0] % 1024))
-    flat = lax.psum(flat, "dp")
+    flat = sum_all(flat, "dp")
     results = []
     cut = 0
     for piece in pieces:

time: 810 us -> 528 us (0.65)
  waiting for transfers between devices: 419 us -> 163 us
  blocking collectives: 48.9 us -> 14.9 us
  matrix products: 123 us -> 93.7 us
  starting transfers between devices: 1.42 us -> 20.5 us
  local copies, waits for them, and re-layouts: 100 us -> 113 us
    unnamed x15 -> x6, waiting for transfers between devices: 157 us -> 39.9 us
    ppermute x0 -> x21, waiting for transfers between devices: none -> 79.3 us  [swap(): return lax.ppermute(values, axis, [(i, i ^ bit) for i in range(count)])]
    reduce_scatter x4 -> x0, waiting for transfers between devices: 78.8 us -> none  [scatter_rows(): lax.psum_scatter(values, 'tensor', scatter_dimension=0, tiled=True)]
    all_gather x4 -> x0, waiting for transfers between devices: 63.9 us -> none  [gather_rows(): return lax.all_gather(values, 'tensor', axis=0, tiled=True)]
    psum x1 -> x0, blocking collectives: 35.3 us -> none  [body(): flat = lax.psum(flat, 'dp')]
    psum x1 -> x0, waiting for transfers between devices: 28.6 us -> none  [body(): lax.psum(jnp.concatenate([pair, used_rows[:, 2 * HEAD_SIZE:], small_rows]...]
    all_gather x1, waiting for transfers between devices: 26.3 us -> 0.04 us  [body(): second_all = lax.all_gather(second_pack, 'dp', axis=0, tiled=True)]
    ppermute x0 -> x21, starting transfers between devices: none -> 20 us  [swap(): return lax.ppermute(values, axis, [(i, i ^ bit) for i in range(count)])]
  transfers between devices with their start and end apart: 13 -> 25, of which waited for: 12 -> 17; matrix products, arithmetic and copies ran while one was open for 12% -> 32% of each run, Pallas kernels for 0% -> 0%
where the time goes in v2:
time: 528 us; the launch traced here: 520 us
  waiting for transfers between devices  163 us (31%)
  local copies, waits for them, and re-layouts  113 us (21%)
  other arithmetic  98.4 us (19%)
  matrix products  93.7 us (18%)
  starting transfers between devices  20.5 us (4%)
  between operations  16.9 us (3%)
  blocking collectives  14.9 us (3%)
    ppermute x21, waiting for transfers between devices, swap(): return lax.ppermute(values, axis, [(i, i ^ bit) for i in range(count)])  79.3 us
    unnamed x425, local copies, waits for them, and re-layouts  54.8 us
    all_gather x1, waiting for transfers between devices, body(): first_all = lax.all_gather(first_pack, 'dp', axis=0, tiled=True)  43.8 us
    unnamed x6, waiting for transfers between devices  39.9 us
    dot_general x10, matrix products, dot(): return jnp.dot(left, right, preferred_element_type=f32)  21 us
    ppermute x21, starting transfers between devices, swap(): return lax.ppermute(values, axis, [(i, i ^ bit) for i in range(count)])  20 us
    dot_general x8, matrix products, dot_t(): lax.dot_general(left, right, (((1,), (1,)), ((), ())), preferred_element_...  16.7 us
    dot_general x3, matrix products, state_scan(): jnp.einsum('clrh,crhp->clhp', mixing, inner_blocks, precision=highest_pre...  14.2 us
  transfers between devices with their start and end apart: 25, of which 17 were waited for; matrix products, arithmetic and copies ran while one was open for 32% of the time, Pallas kernels for 0%

profile of v2, /device:TPU:0, one launch (start us, length us, event | category | flops | bytes accessed | tf_op | source)
XLA Modules:
  0.0 520.0 jit_solution(74751288386052464)
XLA Ops:
  11.9 3.0 collective-permute-start
  21.1 6.0 %collective-permute-done = bf16[1,256,1024]{2,1,0:T(8,128)(2,1)S(1)} collective-permute-done((bf16[1,256,1024]{2,1,0:T(8,128)(2,1)}, bf16[1,256,1024]{2,1,0:T(8,128)(2,1)S(1)}, u32[]{:S(2)}, u32[]{:S(2)}) %collective-permute-start) | collective-permute-done | bytes 524320 | tf_op jit(solution)/shard_map/ppermute | solution.py:182
  34.0 43.8 %all-gather.3.cloned.1.call-done = bf16[1024,1536]{0,1:T(8,128)(2,1)} async-done(((bf16[128,1536]{0,1:T(8,128)(2,1)}), bf16[1024,1536]{0,1:T(8,128)(2,1)}) %all-gather.3.cloned.1.call-update) | async-done | bytes 3145744 | tf_op jit(solution)/shard_map/all_gather | solution.py:295
  80.0 1.9 slice.319
  81.9 1.9 multiply_convert_fusion.1
  91.5 3.8 fusion.114
  95.3 2.2 fusion.233
  103.5 2.4 fusion.227
  109.6 5.8 %multiply_convert_fusion.6 = (bf16[1024,384]{1,0:T(8,128)(2,1)}, f32[1024,384]{1,0:T(8,128)}) fusion(f32[1024,384]{1,0:T(8,128)} %fusion.114, f32[384]{0:T(512)S(1)} %copy-done.124, f32[384]{0:T(512)S(1)} %copy-done.126, f32[384]{0:T(512)S(1)} %copy-done.128, f32[384]{0:T(512)S(1)} %copy-done.130, f32[384]{0:T(512)S(1)} %copy-done.175), kind=kLoop, calls=%fused_computation.123 | loop fusion | flops 5111808 | bytes 3939840 | tf_op jit(solution)/shard_map/convert_element_type | solution.py:365
  115.5 2.4 copy.293
  117.8 2.2 copy.394
  120.1 1.9 copy.381
  122.0 4.2 multiply_convert_fusion.8
  129.9 3.5 bitcast_add_fusion.1
  135.8 3.1 copy.304
  149.3 3.2 multiply_reduce_fusion.11
  153.0 6.7 %psum.14 = f32[1024]{0:T(1024)} all-reduce(f32[1024]{0:T(1024)S(1)} %get-tuple-element.184), channel_id=1, replica_groups=mesh['dp'=8,'tensor'=4] {'tensor'}, use_global_device_ids=true, to_apply=%region_7.8 | all-reduce | flops 1024 | bytes 8192 | tf_op jit(solution)/shard_map/psum | solution.py:380
  159.7 3.2 convolution_convert_fusion.9
  166.7 3.1 fusion.87
  173.5 2.4 add_convert_fusion
  178.3 2.9 collective-permute-done.4
  185.7 12.6 %collective-permute-done.5 = bf16[1,256,1024]{2,1,0:T(8,128)(2,1)} collective-permute-done((bf16[1,256,1024]{2,1,0:T(8,128)(2,1)S(1)}, bf16[1,256,1024]{2,1,0:T(8,128)(2,1)}, u32[]{:S(2)}, u32[]{:S(2)}) %collective-permute-start.5) | collective-permute-done | bytes 524320 | tf_op jit(solution)/shard_map/ppermute | solution.py:182
  198.3 2.4 multiply_reduce_fusion.17
  202.5 11.7 %collective-permute-done.6 = bf16[1,256,1024]{2,1,0:T(8,128)(2,1)S(1)} collective-permute-done((bf16[1,256,1024]{2,1,0:T(8,128)(2,1)S(1)}, bf16[1,256,1024]{2,1,0:T(8,128)(2,1)S(1)}, u32[]{:S(2)}, u32[]{:S(2)}) %collective-permute-start.6) | collective-permute-done | bytes 524320 | tf_op jit(solution)/shard_map/ppermute | solution.py:182
  219.1 2.2 multiply_convert_fusion.4
  221.3 2.6 fusion.28
  224.2 2.5 collective-permute-done.8
  228.7 12.5 %collective-permute-done.9 = bf16[1,256,1024]{2,1,0:T(8,128)(2,1)S(1)} collective-permute-done((bf16[1,256,1024]{2,1,0:T(8,128)(2,1)S(1)}, bf16[1,256,1024]{2,1,0:T(8,128)(2,1)S(1)}, u32[]{:S(2)}, u32[]{:S(2)}) %collective-permute-start.9) | collective-permute-done | bytes 524320 | tf_op jit(solution)/shard_map/ppermute | solution.py:182
  246.7 9.6 %collective-permute-done.10 = bf16[1,256,1024]{2,1,0:T(8,128)(2,1)S(1)} collective-permute-done((bf16[1,256,1024]{2,1,0:T(8,128)(2,1)S(1)}, bf16[1,256,1024]{2,1,0:T(8,128)(2,1)S(1)}, u32[]{:S(2)}, u32[]{:S(2)}) %collective-permute-start.10) | collective-permute-done | bytes 524320 | tf_op jit(solution)/shard_map/ppermute | solution.py:182
  256.6 2.6 convolution_convert_fusion.1
  260.5 2.3 convolution_convert_fusion
  266.6 2.3 pad_maximum_fusion
  268.9 3.1 multiply_reduce_fusion.4
  271.9 8.3 %psum.15 = f32[1024]{0:T(1024)} all-reduce(f32[1024]{0:T(1024)} %get-tuple-element.143), channel_id=1, replica_groups=mesh['dp'=8,'tensor'=4] {'tensor'}, use_global_device_ids=true, to_apply=%region_11.12 | all-reduce | flops 1024 | bytes 8192 | tf_op jit(solution)/shard_map/psum | solution.py:434
  280.9 5.4 %fusion.35 = (f32[384]{0:T(512)}, f32[1024,384]{1,0:T(8,128)}, bf16[1024,384]{1,0:T(8,128)(2,1)}) fusion(bf16[1024,384]{1,0:T(8,128)(2,1)} %get-tuple-element.192, f32[1024,384]{1,0:T(8,128)} %get-tuple-element.281, f32[1024]{0:T(1024)S(1)} %broadcast_multiply_fusion.9, f32[1024,384]{1,0:T(8,128)} %get-tuple-element.185, f32[1024,384]{1,0:T(8,128)} %get-tuple-element.282, ...), kind=kLoop, calls=%fused_computation.78 | loop fusion | flops 9043584 | bytes 9449984 | tf_op jit(solution)/shard_map/transpose(jvp())/reduce_sum | solution.py:102
  286.3 3.1 copy.310
  292.6 3.7 fusion.74
  299.1 3.5 fusion.70
  303.7 6.0 %fusion.32 = (f32[8,128,6]{1,2,0:T(8,128)}, f32[8,128,6]{1,2,0:T(8,128)}, f32[8,128,6]{1,2,0:T(8,128)}, f32[8,128,128]{2,1,0:T(8,128)}) fusion(f32[8,128,6]{1,2,0:T(8,128)S(1)} %copy-done.120, f32[8,128,6]{1,2,0:T(8,128)S(1)} %copy-done.118, f32[8,128,128]{2,1,0:T(8,128)S(1)} %copy-done.91, pred[128,128]{1,0:T(8,128)(4,1)S(1)} %copy-done.149, ...), kind=kOutput, calls=%fused_computation.74 | convolution fusion | flops 614053888 | bytes 3547136 | tf_op jit(solution)/shard_map/transpose(jvp(clrh,crhp->clhp))/dot_general | solution.py:85
  311.2 4.7 bitcast_add_fusion
  316.0 6.5 %copy.377 = bf16[1024,2048]{1,0:T(8,128)(2,1)} copy(bf16[1024,2048]{0,1:T(8,128)(2,1)} %pad_maximum_fusion) | data formatting | bytes 8388608
  322.8 2.3 dynamic-slice_bitcast_fusion.1
  332.2 2.8 fusion.156
  341.9 3.1 copy.314
  345.0 4.8 multiply_reduce_fusion.14
  351.0 2.6 fusion.225
  353.7 2.1 fusion.126
  355.8 1.9 copy.337
  359.5 2.6 convolution_convert_fusion.8
  374.7 2.2 fusion.82
  393.1 2.8 fusion.175
  395.9 9.1 %collective-permute-done.13 = bf16[1,256,1024]{2,1,0:T(8,128)(2,1)S(1)} collective-permute-done((bf16[1,256,1024]{2,1,0:T(8,128)(2,1)S(1)}, bf16[1,256,1024]{2,1,0:T(8,128)(2,1)S(1)}, u32[]{:S(2)}, u32[]{:S(2)}) %collective-permute-start.13) | collective-permute-done | bytes 524320 | tf_op jit(solution)/shard_map/ppermute | solution.py:182
  408.0 2.0 copy.378
  410.1 3.4 convolution_convert_fusion.2
  419.8 1.9 multiply_reduce_fusion
  421.9 1.9 pad_maximum_fusion.1
  423.8 4.8 copy.379
  437.1 2.2 collective-permute-start.20
  439.3 3.1 collective-permute-done.20
  447.4 2.0 convert_add_fusion
  455.3 2.2 add_convert_fusion.1
  457.5 3.6 collective-permute-done.15
  462.4 38.0 %reduce-scatter.9.cloned.1.call-done = bf16[128,1408]{1,0:T(8,128)(2,1)} async-done(((bf16[1024,1408]{1,0:T(8,128)(2,1)}), bf16[128,1408]{1,0:T(8,128)(2,1)}) %reduce-scatter.9.cloned.1.call-update) | async-done | bytes 360464
  505.7 2.7 fusion.92
  (666 shorter events, 181.8 us)
Async XLA Ops:
  7.2 19.9 %copy-start.22 = (bf16[256,1024]{1,0:T(8,128)(2,1)S(1)}, bf16[256,1024]{1,0:T(8,128)(2,1)}, u32[]{:S(2)}) copy-start(bf16[256,1024]{1,0:T(8,128)(2,1)} %param.18) | copy-start | bytes 1572868
  7.2 11.8 %copy-start.99 = (bf16[128,2,512]{2,1,0:T(2,128)(2,1)S(1)}, bf16[128,2,512]{2,1,0:T(2,128)(2,1)}, u32[]{:S(2)}) copy-start(bf16[128,2,512]{2,1,0:T(2,128)(2,1)} %param.34) | copy-start | bytes 786436
  7.2 70.6 %all-gather.3.cloned.1.call-start = ((), (), s32[]{:S(2)}) async-start(), calls=%async_computation.2 | async-start | bytes 3538944 | tf_op jit(solution)/shard_map/all_gather | solution.py:295
  11.9 159.8 %all-gather.5.cloned.1.call-start = ((), (), s32[]{:S(2)}) async-start(), calls=%async_computation.3 | async-start | bytes 4718592 | tf_op jit(solution)/shard_map/all_gather | solution.py:299
  11.9 15.2 %collective-permute-start = (bf16[1,256,1024]{2,1,0:T(8,128)(2,1)}, bf16[1,256,1024]{2,1,0:T(8,128)(2,1)S(1)}, u32[]{:S(2)}, u32[]{:S(2)}) collective-permute-start(bf16[1,256,1024]{2,1,0:T(8,128)(2,1)} %bitcast.585), channel_id=1, source_target_pairs={{0,2},{1,3},{2,0},{3,1},{4,6},{5,7},{6,4},{7,5},{8,10},{9,11},{10,... | collective-permute-start | bytes 1572872 | tf_op jit(solution)/shard_map/ppermute | solution.py:182
  19.1 9.0 %copy-start.181 = (f32[32]{0:T(128)}, f32[32]{0:T(128)S(1)}, u32[]{:S(2)}) copy-start(f32[32]{0:T(128)S(1)} %multiply_power_fusion) | copy-start | bytes 388
  21.1 7.0 %copy-start.195 = (bf16[6]{0:T(256)(128)(2,1)S(1)}, bf16[6]{0:T(256)(128)(2,1)}, u32[]{:S(2)}) copy-start(bf16[6]{0:T(256)(128)(2,1)} %param.29) | copy-start | bytes 40
  21.1 8.2 %copy-start.104 = (bf16[128,512]{1,0:T(8,128)(2,1)S(1)}, bf16[128,512]{1,0:T(8,128)(2,1)}, u32[]{:S(2)}) copy-start(bf16[128,512]{1,0:T(8,128)(2,1)} %param.35) | copy-start | bytes 393220
  21.1 8.2 %copy-start.113 = (bf16[128,384]{1,0:T(8,128)(2,1)S(1)}, bf16[128,384]{1,0:T(8,128)(2,1)}, u32[]{:S(2)}) copy-start(bf16[128,384]{1,0:T(8,128)(2,1)} %param.32) | copy-start | bytes 294916
  21.1 8.2 %copy-start.116 = (bf16[128,128]{1,0:T(8,128)(2,1)S(1)}, bf16[128,128]{1,0:T(8,128)(2,1)}, u32[]{:S(2)}) copy-start(bf16[128,128]{1,0:T(8,128)(2,1)} %param.23) | copy-start | bytes 98308
  27.3 4.1 collective-permute-start.1
  28.1 56.7 %copy-start.185 = (f32[6]{0:T(128)}, f32[6]{0:T(128)S(1)}, u32[]{:S(2)}) copy-start(f32[6]{0:T(128)S(1)} %fusion.182) | copy-start | bytes 76
  32.8 49.2 %copy-start.2 = (bf16[2,1,256,1024]{3,2,1,0:T(8,128)(2,1)}, bf16[2,1,256,1024]{3,2,1,0:T(8,128)(2,1)S(1)}, u32[]{:S(2)}) copy-start(bf16[2,1,256,1024]{3,2,1,0:T(8,128)(2,1)S(1)} %get-tuple-element.211) | copy-start | bytes 3145732
  32.8 107.6 %copy-start = (bf16[2,1,256,1024]{3,2,1,0:T(8,128)(2,1)}, bf16[2,1,256,1024]{3,2,1,0:T(8,128)(2,1)S(1)}, u32[]{:S(2)}) copy-start(bf16[2,1,256,1024]{3,2,1,0:T(8,128)(2,1)S(1)} %get-tuple-element.210) | copy-start | bytes 3145732
  34.0 49.8 %copy-start.114 = (f32[2,2,2,128]{3,1,2,0:T(2,128)}, f32[2,2,2,128]{3,1,2,0:T(2,128)S(1)}, u32[]{:S(2)}) copy-start(f32[2,2,2,128]{3,1,2,0:T(2,128)S(1)} %copy.392) | copy-start | bytes 12292
  78.6 61.8 %copy-start.107 = (f32[1024,1]{0,1:T(1,128)}, f32[1024,1]{0,1:T(1,128)S(1)}, u32[]{:S(2)}) copy-start(f32[1024,1]{0,1:T(1,128)S(1)} %get-tuple-element.203) | copy-start | bytes 12292
  84.8 6.7 %copy-start.97 = (f32[1024,6]{0,1:T(8,128)}, f32[1024,6]{0,1:T(8,128)S(1)}, u32[]{:S(2)}) copy-start(f32[1024,6]{0,1:T(8,128)S(1)} %convolution_add_fusion.2) | copy-start | bytes 73732
  99.9 9.7 %copy-start.124 = (f32[384]{0:T(512)S(1)}, f32[384]{0:T(512)}, u32[]{:S(2)}) copy-start(f32[384]{0:T(512)} %get-tuple-element.159) | copy-start | bytes 4612
  99.9 9.7 %copy-start.126 = (f32[384]{0:T(512)S(1)}, f32[384]{0:T(512)}, u32[]{:S(2)}) copy-start(f32[384]{0:T(512)} %get-tuple-element.160) | copy-start | bytes 4612
  99.9 9.7 %copy-start.128 = (f32[384]{0:T(512)S(1)}, f32[384]{0:T(512)}, u32[]{:S(2)}) copy-start(f32[384]{0:T(512)} %get-tuple-element.161) | copy-start | bytes 4612
  99.9 9.7 %copy-start.130 = (f32[384]{0:T(512)S(1)}, f32[384]{0:T(512)}, u32[]{:S(2)}) copy-start(f32[384]{0:T(512)} %get-tuple-element.162) | copy-start | bytes 4612
  99.9 9.7 %copy-start.175 = (f32[384]{0:T(512)S(1)}, f32[384]{0:T(512)}, u32[]{:S(2)}) copy-start(f32[384]{0:T(512)} %get-tuple-element.158) | copy-start | bytes 4612
  100.0 308.0 %reduce-scatter.7.cloned.1.call-start = ((), (), s32[]{:S(2)}) async-start(), calls=%async_computation.4 | async-start | bytes 4718592
  100.2 21.7 %copy-start.167 = (f32[1,256]{1,0:T(1,128)}, f32[1,256]{1,0:T(1,128)S(1)}, u32[]{:S(2)}) copy-start(f32[1,256]{1,0:T(1,128)S(1)} %get-tuple-element.266) | copy-start | bytes 3076
  100.3 21.7 %copy-start.169 = (f32[1,256]{1,0:T(1,128)}, f32[1,256]{1,0:T(1,128)S(1)}, u32[]{:S(2)}) copy-start(f32[1,256]{1,0:T(1,128)S(1)} %get-tuple-element.267) | copy-start | bytes 3076
  100.3 21.7 %copy-start.171 = (f32[1,256]{1,0:T(1,128)}, f32[1,256]{1,0:T(1,128)S(1)}, u32[]{:S(2)}) copy-start(f32[1,256]{1,0:T(1,128)S(1)} %get-tuple-element.268) | copy-start | bytes 3076
  100.3 21.7 %copy-start.173 = (f32[1,256]{1,0:T(1,128)}, f32[1,256]{1,0:T(1,128)S(1)}, u32[]{:S(2)}) copy-start(f32[1,256]{1,0:T(1,128)S(1)} %get-tuple-element.269) | copy-start | bytes 3076
  100.3 62.6 %collective-permute-start.2 = (bf16[1,256,1024]{2,1,0:T(8,128)(2,1)}, bf16[1,256,1024]{2,1,0:T(8,128)(2,1)}, u32[]{:S(2)}, u32[]{:S(2)}) collective-permute-start(bf16[1,256,1024]{2,1,0:T(8,128)(2,1)} %bitcast.622), channel_id=1, source_target_pairs={{0,2},{1,3},{2,0},{3,1},{4,6},{5,7},{6,4},{7,5},{8,10},{9,11},{10,... | collective-permute-start | bytes 1572872 | tf_op jit(solution)/shard_map/ppermute | solution.py:182
  103.5 24.5 %copy-start.121 = (f32[6]{0:T(128)}, f32[6]{0:T(128)S(1)}, u32[]{:S(2)}) copy-start(f32[6]{0:T(128)S(1)} %get-tuple-element.263) | copy-start | bytes 76
  115.5 6.6 %copy-start.184 = (f32[256,1]{0,1:T(1,128)S(1)}, f32[256,1]{0,1:T(1,128)}, u32[]{:S(2)}) copy-start(f32[256,1]{0,1:T(1,128)} %slice.426) | copy-start | bytes 3076
  144.4 8.1 %copy-start.18 = (f32[512,512,2]{1,0,2:T(8,128)}, f32[512,512,2]{1,0,2:T(8,128)S(1)}, u32[]{:S(2)}) copy-start(f32[512,512,2]{1,0,2:T(8,128)S(1)} %get-tuple-element.280) | copy-start | bytes 6291460
  144.4 15.3 %copy-start.138 = (f32[2,512]{1,0:T(2,128)}, f32[2,512]{1,0:T(2,128)S(1)}, u32[]{:S(2)}) copy-start(f32[2,512]{1,0:T(2,128)S(1)} %get-tuple-element.279) | copy-start | bytes 12292
  153.0 9.8 %copy-start.145 = (f32[2,512]{1,0:T(2,128)}, f32[2,512]{1,0:T(2,128)S(1)}, u32[]{:S(2)}) copy-start(f32[2,512]{1,0:T(2,128)S(1)} %fusion.33) | copy-start | bytes 12292
  164.3 5.5 %collective-permute-start.3 = (bf16[2,256,1024]{2,1,0:T(8,128)(2,1)S(1)}, bf16[2,256,1024]{2,1,0:T(8,128)(2,1)S(1)}, u32[]{:S(2)}, u32[]{:S(2)}) collective-permute-start(bf16[2,256,1024]{2,1,0:T(8,128)(2,1)S(1)} %maximum_bitcast_fusion.1), channel_id=1, source_target_pairs={{0,1},{1,0},{2,3},{3,2},{4,5},{5,4},{6,7},{7,6},{8,9},{9,8},{10,11... | collective-permute-start | bytes 3145736 | tf_op jit(solution)/shard_map/ppermute | solution.py:182
  178.3 2.9 collective-permute-start.4
  184.2 14.1 %collective-permute-start.5 = (bf16[1,256,1024]{2,1,0:T(8,128)(2,1)S(1)}, bf16[1,256,1024]{2,1,0:T(8,128)(2,1)}, u32[]{:S(2)}, u32[]{:S(2)}) collective-permute-start(bf16[1,256,1024]{2,1,0:T(8,128)(2,1)S(1)} %dynamic-slice_convert_fusion.3), channel_id=1, source_target_pairs={{0,2},{1,3},{2,0},{3,1},{4,6},{5,7},{6,4},{7,5},{8,10},{9,11},{10,... | collective-permute-start | bytes 1572872 | tf_op jit(solution)/shard_map/ppermute | solution.py:182
  200.8 13.9 %copy-start.94 = (bf16[1024,2048]{1,0:T(8,128)(2,1)S(1)}, bf16[1024,2048]{1,0:T(8,128)(2,1)}, u32[]{:S(2)}) copy-start(bf16[1024,2048]{1,0:T(8,128)(2,1)} %all-gather.5.cloned.1.call-done) | copy-start | bytes 12582916
  200.9 13.7 %copy-start.62 = (bf16[2,2,256,1024]{3,2,1,0:T(8,128)(2,1)S(1)}, bf16[2,2,256,1024]{3,2,1,0:T(8,128)(2,1)}, u32[]{:S(2)}) copy-start(bf16[2,2,256,1024]{3,2,1,0:T(8,128)(2,1)} %copy.305) | copy-start | bytes 6291460
  201.0 13.2 %collective-permute-start.6 = (bf16[1,256,1024]{2,1,0:T(8,128)(2,1)S(1)}, bf16[1,256,1024]{2,1,0:T(8,128)(2,1)S(1)}, u32[]{:S(2)}, u32[]{:S(2)}) collective-permute-start(bf16[1,256,1024]{2,1,0:T(8,128)(2,1)S(1)} %fusion.121), channel_id=1, source_target_pairs={{0,2},{1,3},{2,0},{3,1},{4,6},{5,7},{6,4},{7,5},{8,10},{9,11},{10,... | collective-permute-start | bytes 1572872 | tf_op jit(solution)/shard_map/ppermute | solution.py:182
  214.6 2.7 collective-permute-start.7
  224.0 2.7 collective-permute-start.8
  227.1 14.6 %copy-start.67 = (bf16[256,1024]{1,0:T(8,128)(2,1)S(1)}, bf16[256,1024]{1,0:T(8,128)(2,1)}, u32[]{:S(2)}) copy-start(bf16[256,1024]{1,0:T(8,128)(2,1)} %param.19) | copy-start | bytes 1572868
  227.2 14.0 %collective-permute-start.9 = (bf16[1,256,1024]{2,1,0:T(8,128)(2,1)S(1)}, bf16[1,256,1024]{2,1,0:T(8,128)(2,1)S(1)}, u32[]{:S(2)}, u32[]{:S(2)}) collective-permute-start(bf16[1,256,1024]{2,1,0:T(8,128)(2,1)S(1)} %dynamic-slice_convert_fusion.2), channel_id=1, source_target_pairs={{0,2},{1,3},{2,0},{3,1},{4,6},{5,7},{6,4},{7,5},{8,10},{9,11},{10,... | collective-permute-start | bytes 1572872 | tf_op jit(solution)/shard_map/ppermute | solution.py:182
  243.2 13.1 %collective-permute-start.10 = (bf16[1,256,1024]{2,1,0:T(8,128)(2,1)S(1)}, bf16[1,256,1024]{2,1,0:T(8,128)(2,1)S(1)}, u32[]{:S(2)}, u32[]{:S(2)}) collective-permute-start(bf16[1,256,1024]{2,1,0:T(8,128)(2,1)S(1)} %get-tuple-element.180), channel_id=1, source_target_pairs={{0,2},{1,3},{2,0},{3,1},{4,6},{5,7},{6,4},{7,5},{8,10},{9,11},{10,... | collective-permute-start | bytes 1572872 | tf_op jit(solution)/shard_map/ppermute | solution.py:182
  256.6 6.9 %collective-permute-start.11 = (bf16[2,256,1024]{2,1,0:T(8,128)(2,1)S(1)}, bf16[2,256,1024]{2,1,0:T(8,128)(2,1)S(1)}, u32[]{:S(2)}, u32[]{:S(2)}) collective-permute-start(bf16[2,256,1024]{2,1,0:T(8,128)(2,1)S(1)} %maximum_bitcast_fusion.3), channel_id=1, source_target_pairs={{0,1},{1,0},{2,3},{3,2},{4,5},{5,4},{6,7},{7,6},{8,9},{9,8},{10,11... | collective-permute-start | bytes 3145736 | tf_op jit(solution)/shard_map/ppermute | solution.py:182
  268.8 12.1 %copy-start.135 = (f32[384]{0:T(512)S(1)}, f32[384]{0:T(512)}, u32[]{:S(2)}) copy-start(f32[384]{0:T(512)} %mul.1141) | copy-start | bytes 4612
  322.5 177.9 %reduce-scatter.9.cloned.1.call-start = ((), (), s32[]{:S(2)}) async-start(), calls=%async_computation.5 | async-start | bytes 3244032
  322.8 9.4 %copy-start.161 = (f32[6]{0:T(128)S(1)}, f32[6]{0:T(128)}, u32[]{:S(2)}) copy-start(f32[6]{0:T(128)} %get-tuple-element.265) | copy-start | bytes 76
  325.0 63.0 %collective-permute-start.12 = (bf16[2,256,1024]{2,1,0:T(8,128)(2,1)}, bf16[2,256,1024]{2,1,0:T(8,128)(2,1)}, u32[]{:S(2)}, u32[]{:S(2)}) collective-permute-start(bf16[2,256,1024]{2,1,0:T(8,128)(2,1)} %dynamic-slice_bitcast_fusion.1), channel_id=1, source_target_pairs={{0,1},{1,0},{2,3},{3,2},{4,5},{5,4},{6,7},{7,6},{8,9},{9,8},{10,11... | collective-permute-start | bytes 3145736 | tf_op jit(solution)/shard_map/ppermute | solution.py:182
  355.8 6.4 %copy-start.54 = (pred[512,512]{0,1:T(8,128)(4,1)S(1)}, pred[512,512]{0,1:T(8,128)(4,1)}, u32[]{:S(2)}) copy-start(pred[512,512]{0,1:T(8,128)(4,1)} %iota_compare_fusion.1) | copy-start | bytes 786436
  355.8 6.4 %copy-start.151 = (f32[2,512]{1,0:T(2,128)S(1)}, f32[2,512]{1,0:T(2,128)}, u32[]{:S(2)}) copy-start(f32[2,512]{1,0:T(2,128)} %log_add_fusion.1) | copy-start | bytes 12292
  390.8 14.3 %collective-permute-start.13 = (bf16[1,256,1024]{2,1,0:T(8,128)(2,1)S(1)}, bf16[1,256,1024]{2,1,0:T(8,128)(2,1)S(1)}, u32[]{:S(2)}, u32[]{:S(2)}) collective-permute-start(bf16[1,256,1024]{2,1,0:T(8,128)(2,1)S(1)} %dynamic-slice_convert_fusion.1), channel_id=1, source_target_pairs={{0,2},{1,3},{2,0},{3,1},{4,6},{5,7},{6,4},{7,5},{8,10},{9,11},{10,... | collective-permute-start | bytes 1572872 | tf_op jit(solution)/shard_map/ppermute | solution.py:182
  421.8 9.4 %copy-start.25 = (bf16[1024,1024]{1,0:T(8,128)(2,1)}, bf16[1024,1024]{1,0:T(8,128)(2,1)S(1)}, u32[]{:S(2)}) copy-start(bf16[1024,1024]{1,0:T(8,128)(2,1)S(1)} %get-tuple-element.198) | copy-start | bytes 6291460
  428.6 10.7 %copy-start.183 = (f32[256]{0:T(256)S(1)}, f32[256]{0:T(256)}, u32[]{:S(2)}) copy-start(f32[256]{0:T(256)} %get-tuple-element.236) | copy-start | bytes 3076
  429.7 3.7 collective-permute-start.18
  432.2 15.2 %collective-permute-start.14 = (bf16[2,256,1024]{2,1,0:T(8,128)(2,1)}, bf16[2,256,1024]{2,1,0:T(8,128)(2,1)}, u32[]{:S(2)}, u32[]{:S(2)}) collective-permute-start(bf16[2,256,1024]{2,1,0:T(8,128)(2,1)} %dynamic-slice_bitcast_fusion), channel_id=1, source_target_pairs={{0,1},{1,0},{2,3},{3,2},{4,5},{5,4},{6,7},{7,6},{8,9},{9,8},{10,11... | collective-permute-start | bytes 3145736 | tf_op jit(solution)/shard_map/ppermute | solution.py:182
  433.4 3.7 collective-permute-start.19
  437.1 5.3 %collective-permute-start.20 = (f32[3072]{0:T(1024)S(1)}, f32[3072]{0:T(1024)S(1)}, u32[]{:S(2)}, u32[]{:S(2)}) collective-permute-start(f32[3072]{0:T(1024)S(1)} %add.517), channel_id=1, source_target_pairs={{0,16},{4,20},{8,24},{12,28},{16,0},{20,4},{24,8},{28,12},{1,17},{... | collective-permute-start | bytes 36872 | tf_op jit(solution)/shard_map/ppermute | solution.py:182
  447.4 6.9 %slice-start = ((bf16[128,2048]{0,1:T(8,128)(2,1)}), bf16[128,1024]{0,1:T(8,128)(2,1)S(1)}, s32[]{:S(2)}) async-start(bf16[128,2048]{0,1:T(8,128)(2,1)} %copy.378), calls=%async_computation.6 | async-start | bytes 524288 | tf_op jit(solution)/shard_map/slice | solution.py:526
  450.4 10.7 %copy-start.108 = (f32[1024,1]{0,1:T(1,128)S(1)}, f32[1024,1]{0,1:T(1,128)}, u32[]{:S(2)}) copy-start(f32[1024,1]{0,1:T(1,128)} %copy-done.107) | copy-start | bytes 12292
  450.4 10.7 %collective-permute-start.15 = (bf16[1,256,1024]{2,1,0:T(8,128)(2,1)}, bf16[1,256,1024]{2,1,0:T(8,128)(2,1)}, u32[]{:S(2)}, u32[]{:S(2)}) collective-permute-start(bf16[1,256,1024]{2,1,0:T(8,128)(2,1)} %dynamic-slice_convert_fusion), channel_id=1, source_target_pairs={{0,2},{1,3},{2,0},{3,1},{4,6},{5,7},{6,4},{7,5},{8,10},{9,11},{10,... | collective-permute-start | bytes 1572872 | tf_op jit(solution)/shard_map/ppermute | solution.py:182
  457.5 48.2 %copy-start.24 = (bf16[256,1024]{1,0:T(8,128)(2,1)S(1)}, bf16[256,1024]{1,0:T(8,128)(2,1)}, u32[]{:S(2)}) copy-start(bf16[256,1024]{1,0:T(8,128)(2,1)} %param.18) | copy-start | bytes 1572868
  502.6 1.5 collective-permute-start.16
  504.1 6.9 %collective-permute-start.17 = (bf16[128,640]{0,1:T(8,128)(2,1)S(1)}, bf16[128,640]{0,1:T(8,128)(2,1)S(1)}, u32[]{:S(2)}, u32[]{:S(2)}) collective-permute-start(bf16[128,640]{0,1:T(8,128)(2,1)S(1)} %fusion.219), channel_id=1, source_target_pairs={{0,2},{1,3},{2,0},{3,1},{4,6},{5,7},{6,4},{7,5},{8,10},{9,11},{10,... | collective-permute-start | bytes 491528 | tf_op jit(solution)/shard_map/ppermute | solution.py:182
  (164 other events, 398.8 us)
Sparse Core Ops, SparseCore 0:
  12.0 65.7 all-gather.2
  100.1 71.5 all-gather.4
  322.7 85.3 reduce-scatter.6
  428.8 71.6 reduce-scatter.8

commit v3 on v2

--- a/solution.py
+++ b/solution.py
@@ -199,25 +199,27 @@
     return held.reshape(count * rows, width)
 
 
-def scatter_rows(values):
-    count = lax.axis_size("tensor")
-    if count & (count - 1):
-        return lax.psum_scatter(values, "tensor", scatter_dimension=0, tiled=True).astype(
-            jnp.float32
-        )
-    index = lax.axis_index("tensor")
-    rows = values.shape[0] // count
-    width = values.shape[1]
-    total = values.reshape(count, rows, width)
-    bit = 1
-    while bit < count:
+def scatter_bits(total, axis, bits):
+    count = lax.axis_size(axis)
+    index = lax.axis_index(axis)
+    rows, width = total.shape[1:]
+    for bit in bits:
         pairs = total.reshape(-1, 2, rows, width)
         mine = (index // bit) % 2
         kept = lax.dynamic_index_in_dim(pairs, mine, 1, keepdims=False)
         sent = lax.dynamic_index_in_dim(pairs, 1 - mine, 1, keepdims=False).astype(jnp.bfloat16)
-        total = kept.astype(jnp.float32) + swap(sent, "tensor", count, bit).astype(jnp.float32)
-        bit *= 2
-    return total.reshape(rows, width)
+        total = kept.astype(jnp.float32) + swap(sent, axis, count, bit).astype(jnp.float32)
+    return total
+
+
+def scatter_rows(values, axis="tensor"):
+    count = lax.axis_size(axis)
+    if count & (count - 1):
+        return lax.psum_scatter(values, axis, scatter_dimension=0, tiled=True).astype(jnp.float32)
+    rows = values.shape[0] // count
+    width = values.shape[1]
+    bits = [1 << k for k in range(count.bit_length() - 1)]
+    return scatter_bits(values.reshape(count, rows, width), axis, bits).reshape(rows, width)
 
 
 def sum_all(values, axis):
@@ -425,7 +427,9 @@
         [back_attention_w, back_mixer_out_w, back_gate_up_w, back_down_w], axis=1
     )
     early, back_mix, down_low = lax.optimization_barrier((early, back_mix, down_low))
-    down_rows = scatter_rows(down_low)
+    tensor_count = lax.axis_size("tensor")
+    down_view = down_low.reshape(tensor_count, sequence_length // tensor_count, width)
+    down_half = scatter_bits(down_view, "tensor", [1])
     early_rows = lax.psum_scatter(early, "dp", scatter_dimension=0, tiled=True)
 
     back_norm = dot(back_mix, mixer_out_all)
@@ -447,6 +451,16 @@
     back_mixer_low = jnp.concatenate([back_gate_z, back_inner_raw], axis=1).astype(bf16)
     back_step_low = back_step_raw.astype(bf16)
     back_mixed_low = dot(back_mix, attention_all).astype(bf16)
+    mixer_grads = t_dot(seq_in, back_mixer_low).astype(bf16)
+    mixer_grads, back_mixed_low, down_half = lax.optimization_barrier(
+        (mixer_grads, back_mixed_low, down_half)
+    )
+    mixer_half = scatter_bits(
+        mixer_grads.reshape(dp_count, own_rows, 2 * channels), "dp", [1]
+    )
+    down_rows = scatter_bits(
+        down_half, "tensor", [1 << k for k in range(1, tensor_count.bit_length() - 1)]
+    ).reshape(inputs.shape)
     back_query_rot, back_keys_rot, back_values = attend_back(
         query_low, keys_reduced, values_reduced, log_total, back_mixed_low, QB
     )
@@ -459,9 +473,12 @@
     back_used_low = jnp.concatenate([back_keys, back_values, back_state_raw], axis=1).astype(bf16)
     used_width = back_used_low.shape[1]
 
-    back_mixer_low, back_query_low, back_used_low, early_rows, down_rows = lax.optimization_barrier(
-        (back_mixer_low, back_query_low, back_used_low, early_rows, down_rows)
-    )
+    back_query_low, back_used_low, early_rows, down_rows, mixer_half = lax.optimization_barrier(
+        (back_query_low, back_used_low, early_rows, down_rows, mixer_half)
+    )
+    mixer_rows = scatter_bits(
+        mixer_half, "dp", [1 << k for k in range(1, dp_count.bit_length() - 1)]
+    ).reshape(own_rows, 2 * channels)
     output = (hidden + down_rows).astype(bf16)
     back_in_part = (
         dot_t(back_query_low, query_all)
@@ -490,28 +507,26 @@
         [
             t_dot(seq_in, back_query_low).astype(bf16),
             t_dot(seq_in, back_used_low).astype(bf16),
-            t_dot(seq_in, back_mixer_low).astype(bf16),
             back_small.astype(bf16),
         ],
         axis=1,
     )
-    late_rows = lax.psum_scatter(late, "dp", scatter_dimension=0, tiled=True)
+    late_rows = scatter_rows(late, "dp")
 
     cut = query_width
-    back_query_w = late_rows[:, :cut].astype(f32)
-    used_rows = late_rows[:, cut : cut + used_width]
+    back_query_w = late_rows[:, :cut]
+    used_rows = late_rows[:, cut : cut + used_width].astype(bf16)
     cut += used_width
-    back_mixer_in_w = late_rows[:, cut : cut + 2 * channels].astype(f32)
-    cut += 2 * channels
     small_rows = late_rows[:, cut:]
-    back_step_w = small_rows[:, :step_heads].astype(f32)
+    back_mixer_in_w = mixer_rows
+    back_step_w = small_rows[:, :step_heads]
     select_heads = (jnp.arange(KEY_VALUE_HEADS) == head_group).astype(bf16)
     pair = (
         used_rows[:, : 2 * HEAD_SIZE].reshape(own_rows, 2, 1, HEAD_SIZE)
         * select_heads[None, None, :, None]
     ).reshape(own_rows, 2 * key_value_width)
     common = sum_all(
-        jnp.concatenate([pair, used_rows[:, 2 * HEAD_SIZE :], small_rows], axis=1), "tensor"
+        jnp.concatenate([pair, used_rows[:, 2 * HEAD_SIZE :], small_rows.astype(bf16)], axis=1), "tensor"
     ).astype(f32)
     back_shared_w = common[:, :shared_width]
     common = common[:, shared_width:]

time: 528 us -> 587 us (1.11)
  local copies, waits for them, and re-layouts: 113 us -> 138 us
  other arithmetic: 98.4 us -> 119 us
  matrix products: 93.7 us -> 103 us
    unnamed x6 -> x4, waiting for transfers between devices: 39.9 us -> 23.8 us
    ppermute x21 -> x27, waiting for transfers between devices: 79.3 us -> 94.8 us  [swap(): return lax.ppermute(values, axis, [(i, i ^ bit) for i in range(count)])]
    add x4 -> x9, other arithmetic: 5.61 us -> 13.6 us  [scatter_bits(): kept.astype(jnp.float32) + swap(sent, axis, count, bit).astype(jnp.float32)]
    convert_element_type x4 -> x8, local copies, waits for them, and re-layouts: 1.1 us -> 7.98 us  [scatter_bits(): lax.dynamic_index_in_dim(pairs, 1 - mine, 1, keepdims=False)]
    ppermute x21 -> x27, starting transfers between devices: 20 us -> 24.2 us  [swap(): return lax.ppermute(values, axis, [(i, i ^ bit) for i in range(count)])]
    unnamed x425 -> x439, local copies, waits for them, and re-layouts: 54.8 us -> 54.5 us
  transfers between devices with their start and end apart: 25 -> 30, of which waited for: 17 -> 18; matrix products, arithmetic and copies ran while one was open for 32% -> 40% of each run, Pallas kernels for 0% -> 0%
where the time goes in v3:
time: 587 us; the launch traced here: 579 us
  waiting for transfers between devices  163 us (28%)
  local copies, waits for them, and re-layouts  138 us (24%)
  other arithmetic  119 us (20%)
  matrix products  103 us (18%)
  starting transfers between devices  24.5 us (4%)
  between operations  16.7 us (3%)
  blocking collectives  14.8 us (3%)
    ppermute x27, waiting for transfers between devices, swap(): return lax.ppermute(values, axis, [(i, i ^ bit) for i in range(count)])  94.8 us
    unnamed x439, local copies, waits for them, and re-layouts  54.5 us
    all_gather x1, waiting for transfers between devices, body(): first_all = lax.all_gather(first_pack, 'dp', axis=0, tiled=True)  43.8 us
    ppermute x27, starting transfers between devices, swap(): return lax.ppermute(values, axis, [(i, i ^ bit) for i in range(count)])  24.2 us
    unnamed x4, waiting for transfers between devices  23.8 us
    dot_general x10, matrix products, dot(): return jnp.dot(left, right, preferred_element_type=f32)  22.9 us
    dot_general x8, matrix products, dot_t(): lax.dot_general(left, right, (((1,), (1,)), ((), ())), preferred_element_...  22.2 us
    dot_general x3, matrix products, state_scan(): jnp.einsum('clrh,crhp->clhp', mixing, inner_blocks, precision=highest_pre...  14.6 us
  transfers between devices with their start and end apart: 30, of which 18 were waited for; matrix products, arithmetic and copies ran while one was open for 40% of the time, Pallas kernels for 0%

profile of v3, /device:TPU:0, one launch (start us, length us, event | category | flops | bytes accessed | tf_op | source)
XLA Modules:
  0.0 579.1 jit_solution(14442505647126471717)
XLA Ops:
  11.9 3.0 collective-permute-start
  21.1 6.0 %collective-permute-done = bf16[1,256,1024]{2,1,0:T(8,128)(2,1)S(1)} collective-permute-done((bf16[1,256,1024]{2,1,0:T(8,128)(2,1)}, bf16[1,256,1024]{2,1,0:T(8,128)(2,1)S(1)}, u32[]{:S(2)}, u32[]{:S(2)}) %collective-permute-start) | collective-permute-done | bytes 524320 | tf_op jit(solution)/shard_map/ppermute | solution.py:182
  34.1 43.8 %all-gather.3.cloned.1.call-done = bf16[1024,1536]{0,1:T(8,128)(2,1)} async-done(((bf16[128,1536]{0,1:T(8,128)(2,1)}), bf16[1024,1536]{0,1:T(8,128)(2,1)}) %all-gather.3.cloned.1.call-update) | async-done | bytes 3145744 | tf_op jit(solution)/shard_map/all_gather | solution.py:297
  91.5 3.7 fusion.114
  103.4 2.3 fusion.232
  109.5 5.9 %multiply_convert_fusion.6 = (bf16[1024,384]{1,0:T(8,128)(2,1)}, f32[1024,384]{1,0:T(8,128)}) fusion(f32[1024,384]{1,0:T(8,128)} %fusion.114, f32[384]{0:T(512)S(1)} %copy-done.133, f32[384]{0:T(512)S(1)} %copy-done.135, f32[384]{0:T(512)S(1)} %copy-done.137, f32[384]{0:T(512)S(1)} %copy-done.139, f32[384]{0:T(512)S(1)} %copy-done.181), kind=kLoop, calls=%fused_computation.123 | loop fusion | flops 5111808 | bytes 3939840 | tf_op jit(solution)/shard_map/convert_element_type | solution.py:367
  115.3 2.4 copy.381
  121.9 4.3 multiply_convert_fusion.8
  129.8 3.5 bitcast_add_fusion.1
  135.7 3.1 copy.392
  149.2 3.1 multiply_reduce_fusion.11
  152.9 6.7 %psum.14 = f32[1024]{0:T(1024)} all-reduce(f32[1024]{0:T(1024)S(1)} %get-tuple-element.212), channel_id=1, replica_groups=mesh['dp'=8,'tensor'=4] {'tensor'}, use_global_device_ids=true, to_apply=%region_7.8 | all-reduce | flops 1024 | bytes 8192 | tf_op jit(solution)/shard_map/psum | solution.py:382
  159.6 3.1 convolution_convert_fusion.9
  166.5 3.1 fusion.87
  173.4 2.4 add_convert_fusion
  178.2 2.9 collective-permute-done.4
  185.7 12.6 %collective-permute-done.5 = bf16[1,256,1024]{2,1,0:T(8,128)(2,1)} collective-permute-done((bf16[1,256,1024]{2,1,0:T(8,128)(2,1)S(1)}, bf16[1,256,1024]{2,1,0:T(8,128)(2,1)}, u32[]{:S(2)}, u32[]{:S(2)}) %collective-permute-start.5) | collective-permute-done | bytes 524320 | tf_op jit(solution)/shard_map/ppermute | solution.py:182
  198.3 2.4 multiply_reduce_fusion.17
  202.4 11.7 %collective-permute-done.6 = bf16[1,256,1024]{2,1,0:T(8,128)(2,1)S(1)} collective-permute-done((bf16[1,256,1024]{2,1,0:T(8,128)(2,1)S(1)}, bf16[1,256,1024]{2,1,0:T(8,128)(2,1)S(1)}, u32[]{:S(2)}, u32[]{:S(2)}) %collective-permute-start.6) | collective-permute-done | bytes 524320 | tf_op jit(solution)/shard_map/ppermute | solution.py:182
  219.1 3.2 multiply_convert_fusion.4
  222.2 2.6 fusion.28
  225.1 2.5 collective-permute-done.8
  235.1 9.4 %collective-permute-done.9 = bf16[1,256,1024]{2,1,0:T(8,128)(2,1)} collective-permute-done((bf16[1,256,1024]{2,1,0:T(8,128)(2,1)}, bf16[1,256,1024]{2,1,0:T(8,128)(2,1)}, u32[]{:S(2)}, u32[]{:S(2)}) %collective-permute-start.9) | collective-permute-done | bytes 524320 | tf_op jit(solution)/shard_map/ppermute | solution.py:182
  246.4 2.5 convert_bitcast_fusion
  252.4 9.6 %collective-permute-done.10 = bf16[1,256,1024]{2,1,0:T(8,128)(2,1)S(1)} collective-permute-done((bf16[1,256,1024]{2,1,0:T(8,128)(2,1)S(1)}, bf16[1,256,1024]{2,1,0:T(8,128)(2,1)S(1)}, u32[]{:S(2)}, u32[]{:S(2)}) %collective-permute-start.10) | collective-permute-done | bytes 524320 | tf_op jit(solution)/shard_map/ppermute | solution.py:182
  262.4 4.1 convolution_convert_fusion.1
  268.6 2.3 convolution_convert_fusion
  274.7 2.3 pad_maximum_fusion
  277.0 4.2 multiply_reduce_fusion.4
  281.2 8.1 %psum.15 = f32[1024]{0:T(1024)} all-reduce(f32[1024]{0:T(1024)} %get-tuple-element.167), channel_id=1, replica_groups=mesh['dp'=8,'tensor'=4] {'tensor'}, use_global_device_ids=true, to_apply=%region_11.12 | all-reduce | flops 1024 | bytes 8192 | tf_op jit(solution)/shard_map/psum | solution.py:438
  290.0 5.3 fusion.35
  295.4 3.0 copy.398
  301.7 3.7 fusion.74
  308.2 3.5 fusion.70
  312.7 6.4 %fusion.32 = (f32[8,128,6]{1,2,0:T(8,128)}, f32[8,128,6]{1,2,0:T(8,128)}, f32[8,128,6]{1,2,0:T(8,128)}, f32[8,128,128]{2,1,0:T(8,128)}) fusion(f32[8,128,6]{1,2,0:T(8,128)S(1)} %copy-done.129, f32[8,128,6]{1,2,0:T(8,128)S(1)} %copy-done.127, f32[8,128,128]{2,1,0:T(8,128)S(1)} %copy-done.100, pred[128,128]{1,0:T(8,128)(4,1)S(1)} %copy-done.156, ...), kind=kOutput, calls=%fused_computation.73 | convolution fusion | flops 614053888 | bytes 3547136 | tf_op jit(solution)/shard_map/transpose(jvp(clrh,crhp->clhp))/dot_general | solution.py:85
  320.6 4.7 bitcast_add_fusion
  326.7 2.3 dynamic-slice_bitcast_fusion.1
  336.1 2.8 fusion.158
  345.8 3.0 copy.402
  348.8 6.7 %multiply_reduce_fusion.8 = (f32[384]{0:T(512)S(1)}, f32[384]{0:T(512)S(1)}, f32[384]{0:T(512)S(1)}, f32[384]{0:T(512)S(1)}, f32[384]{0:T(512)S(1)}, /*index=5*/f32[1024,384]{1,0:T(8,128)}) fusion(f32[1024,384]{1,0:T(8,128)} %fusion.114, f32[1024,384]{1,0:T(8,128)} %get-tuple-element.221, f32[1024,384]{1,0:T(8,128)} %copy.402, ...), kind=kLoop, calls=%fused_computation.98 | loop fusion | flops 7862400 | bytes 7873536 | tf_op jit(solution)/shard_map/transpose(jvp())/reduce_sum | solution.py:52
  356.8 2.6 fusion.230
  365.8 3.8 multiply_reduce_fusion.14
  371.7 6.6 %copy.471 = bf16[1024,2048]{1,0:T(8,128)(2,1)} copy(bf16[1024,2048]{0,1:T(8,128)(2,1)} %pad_maximum_fusion) | data formatting | bytes 8388608
  384.9 2.4 convolution_convert_fusion.8
  387.2 2.8 fusion.177
  390.0 3.9 fusion.42
  393.9 3.1 convolution_convert_fusion.2
  398.1 3.9 collective-permute-done.25
  403.5 3.6 collective-permute-done.26
  408.9 3.3 convert_add_fusion.1
  426.9 2.7 fusion
  436.4 2.3 fusion.82
  447.3 2.4 convert_add_fusion.4
  449.7 23.7 %reduce-scatter.4.cloned.1.call-done = bf16[128,2048]{1,0:T(8,128)(2,1)} async-done(((bf16[1024,2048]{1,0:T(8,128)(2,1)}), bf16[128,2048]{1,0:T(8,128)(2,1)}) %reduce-scatter.4.cloned.1.call-update) | async-done | bytes 524304
  478.9 2.4 fusion.144
  483.1 2.9 multiply_reduce_fusion
  487.3 3.6 reshape_reshape.39
  490.8 4.3 constant_dynamic-slice_fusion.1
  495.1 3.7 copy.478
  498.9 2.8 copy.479
  508.6 9.4 %collective-permute-done.17 = bf16[4,128,640]{2,1,0:T(8,128)(2,1)S(1)} collective-permute-done((bf16[4,128,640]{2,1,0:T(8,128)(2,1)}, bf16[4,128,640]{2,1,0:T(8,128)(2,1)S(1)}, u32[]{:S(2)}, u32[]{:S(2)}) %collective-permute-start.17) | collective-permute-done | bytes 655392 | tf_op jit(solution)/shard_map/ppermute | solution.py:182
  533.1 10.0 %collective-permute-done.19 = bf16[1,128,640]{2,1,0:T(8,128)(2,1)S(1)} collective-permute-done((bf16[1,128,640]{2,1,0:T(8,128)(2,1)S(1)}, bf16[1,128,640]{2,1,0:T(8,128)(2,1)S(1)}, u32[]{:S(2)}, u32[]{:S(2)}) %collective-permute-start.19) | collective-permute-done | bytes 163872 | tf_op jit(solution)/shard_map/ppermute | solution.py:182
  556.6 8.7 %collective-permute-done.21 = bf16[128,640]{1,0:T(8,128)(2,1)} collective-permute-done((bf16[128,640]{1,0:T(8,128)(2,1)}, bf16[128,640]{1,0:T(8,128)(2,1)}, u32[]{:S(2)}, u32[]{:S(2)}) %collective-permute-start.21) | collective-permute-done | bytes 163872 | tf_op jit(solution)/shard_map/ppermute | solution.py:182
  570.0 2.4 fusion.92
  (703 shorter events, 226.9 us)
Async XLA Ops:
  7.2 19.9 %copy-start.24 = (bf16[256,1024]{1,0:T(8,128)(2,1)S(1)}, bf16[256,1024]{1,0:T(8,128)(2,1)}, u32[]{:S(2)}) copy-start(bf16[256,1024]{1,0:T(8,128)(2,1)} %param.18) | copy-start | bytes 1572868
  7.2 11.8 %copy-start.107 = (bf16[128,2,512]{2,1,0:T(2,128)(2,1)S(1)}, bf16[128,2,512]{2,1,0:T(2,128)(2,1)}, u32[]{:S(2)}) copy-start(bf16[128,2,512]{2,1,0:T(2,128)(2,1)} %param.34) | copy-start | bytes 786436
  7.2 70.6 %all-gather.3.cloned.1.call-start = ((), (), s32[]{:S(2)}) async-start(), calls=%async_computation.1 | async-start | bytes 3538944 | tf_op jit(solution)/shard_map/all_gather | solution.py:297
  11.9 159.8 %all-gather.5.cloned.1.call-start = ((), (), s32[]{:S(2)}) async-start(), calls=%async_computation.2 | async-start | bytes 4718592 | tf_op jit(solution)/shard_map/all_gather | solution.py:301
  11.9 15.2 %collective-permute-start = (bf16[1,256,1024]{2,1,0:T(8,128)(2,1)}, bf16[1,256,1024]{2,1,0:T(8,128)(2,1)S(1)}, u32[]{:S(2)}, u32[]{:S(2)}) collective-permute-start(bf16[1,256,1024]{2,1,0:T(8,128)(2,1)} %bitcast.604), channel_id=1, source_target_pairs={{0,2},{1,3},{2,0},{3,1},{4,6},{5,7},{6,4},{7,5},{8,10},{9,11},{10,... | collective-permute-start | bytes 1572872 | tf_op jit(solution)/shard_map/ppermute | solution.py:182
  27.3 4.1 collective-permute-start.1
  28.1 56.7 %copy-start.190 = (f32[6]{0:T(128)}, f32[6]{0:T(128)S(1)}, u32[]{:S(2)}) copy-start(f32[6]{0:T(128)S(1)} %fusion.184) | copy-start | bytes 76
  32.8 49.1 %copy-start.2 = (bf16[2,1,256,1024]{3,2,1,0:T(8,128)(2,1)}, bf16[2,1,256,1024]{3,2,1,0:T(8,128)(2,1)S(1)}, u32[]{:S(2)}) copy-start(bf16[2,1,256,1024]{3,2,1,0:T(8,128)(2,1)S(1)} %get-tuple-element.239) | copy-start | bytes 3145732
  32.8 107.6 %copy-start = (bf16[2,1,256,1024]{3,2,1,0:T(8,128)(2,1)}, bf16[2,1,256,1024]{3,2,1,0:T(8,128)(2,1)S(1)}, u32[]{:S(2)}) copy-start(bf16[2,1,256,1024]{3,2,1,0:T(8,128)(2,1)S(1)} %get-tuple-element.238) | copy-start | bytes 3145732
  34.1 49.8 %copy-start.123 = (f32[2,2,2,128]{3,1,2,0:T(2,128)}, f32[2,2,2,128]{3,1,2,0:T(2,128)S(1)}, u32[]{:S(2)}) copy-start(f32[2,2,2,128]{3,1,2,0:T(2,128)S(1)} %copy.481) | copy-start | bytes 12292
  78.6 61.8 %copy-start.117 = (f32[1024,1]{0,1:T(1,128)}, f32[1024,1]{0,1:T(1,128)S(1)}, u32[]{:S(2)}) copy-start(f32[1024,1]{0,1:T(1,128)S(1)} %get-tuple-element.231) | copy-start | bytes 12292
  99.9 9.6 %copy-start.133 = (f32[384]{0:T(512)S(1)}, f32[384]{0:T(512)}, u32[]{:S(2)}) copy-start(f32[384]{0:T(512)} %get-tuple-element.185) | copy-start | bytes 4612
  99.9 9.6 %copy-start.135 = (f32[384]{0:T(512)S(1)}, f32[384]{0:T(512)}, u32[]{:S(2)}) copy-start(f32[384]{0:T(512)} %get-tuple-element.186) | copy-start | bytes 4612
  99.9 9.6 %copy-start.137 = (f32[384]{0:T(512)S(1)}, f32[384]{0:T(512)}, u32[]{:S(2)}) copy-start(f32[384]{0:T(512)} %get-tuple-element.187) | copy-start | bytes 4612
  99.9 9.6 %copy-start.139 = (f32[384]{0:T(512)S(1)}, f32[384]{0:T(512)}, u32[]{:S(2)}) copy-start(f32[384]{0:T(512)} %get-tuple-element.188) | copy-start | bytes 4612
  99.9 9.6 %copy-start.181 = (f32[384]{0:T(512)S(1)}, f32[384]{0:T(512)}, u32[]{:S(2)}) copy-start(f32[384]{0:T(512)} %get-tuple-element.184) | copy-start | bytes 4612
  99.9 373.5 %reduce-scatter.4.cloned.1.call-start = ((), (), s32[]{:S(2)}) async-start(), calls=%async_computation.3 | async-start | bytes 4718592
  100.2 21.7 %copy-start.173 = (f32[1,256]{1,0:T(1,128)}, f32[1,256]{1,0:T(1,128)S(1)}, u32[]{:S(2)}) copy-start(f32[1,256]{1,0:T(1,128)S(1)} %get-tuple-element.291) | copy-start | bytes 3076
  100.2 21.7 %copy-start.175 = (f32[1,256]{1,0:T(1,128)}, f32[1,256]{1,0:T(1,128)S(1)}, u32[]{:S(2)}) copy-start(f32[1,256]{1,0:T(1,128)S(1)} %get-tuple-element.292) | copy-start | bytes 3076
  100.2 21.7 %copy-start.177 = (f32[1,256]{1,0:T(1,128)}, f32[1,256]{1,0:T(1,128)S(1)}, u32[]{:S(2)}) copy-start(f32[1,256]{1,0:T(1,128)S(1)} %get-tuple-element.293) | copy-start | bytes 3076
  100.2 21.7 %copy-start.179 = (f32[1,256]{1,0:T(1,128)}, f32[1,256]{1,0:T(1,128)S(1)}, u32[]{:S(2)}) copy-start(f32[1,256]{1,0:T(1,128)S(1)} %get-tuple-element.294) | copy-start | bytes 3076
  100.2 62.4 %collective-permute-start.2 = (bf16[1,256,1024]{2,1,0:T(8,128)(2,1)}, bf16[1,256,1024]{2,1,0:T(8,128)(2,1)}, u32[]{:S(2)}, u32[]{:S(2)}) collective-permute-start(bf16[1,256,1024]{2,1,0:T(8,128)(2,1)} %bitcast.644), channel_id=1, source_target_pairs={{0,2},{1,3},{2,0},{3,1},{4,6},{5,7},{6,4},{7,5},{8,10},{9,11},{10,... | collective-permute-start | bytes 1572872 | tf_op jit(solution)/shard_map/ppermute | solution.py:182
  103.4 24.6 %copy-start.130 = (f32[6]{0:T(128)}, f32[6]{0:T(128)S(1)}, u32[]{:S(2)}) copy-start(f32[6]{0:T(128)S(1)} %get-tuple-element.288) | copy-start | bytes 76
  145.4 20.0 %copy-start.147 = (f32[2,512]{1,0:T(2,128)}, f32[2,512]{1,0:T(2,128)S(1)}, u32[]{:S(2)}) copy-start(f32[2,512]{1,0:T(2,128)S(1)} %get-tuple-element.300) | copy-start | bytes 12292
  152.9 9.8 %copy-start.152 = (f32[2,512]{1,0:T(2,128)}, f32[2,512]{1,0:T(2,128)S(1)}, u32[]{:S(2)}) copy-start(f32[2,512]{1,0:T(2,128)S(1)} %fusion.33) | copy-start | bytes 12292
  164.0 5.5 collective-permute-start.3
  178.2 2.9 collective-permute-start.4
  184.1 14.1 %collective-permute-start.5 = (bf16[1,256,1024]{2,1,0:T(8,128)(2,1)S(1)}, bf16[1,256,1024]{2,1,0:T(8,128)(2,1)}, u32[]{:S(2)}, u32[]{:S(2)}) collective-permute-start(bf16[1,256,1024]{2,1,0:T(8,128)(2,1)S(1)} %dynamic-slice_convert_fusion.3), channel_id=1, source_target_pairs={{0,2},{1,3},{2,0},{3,1},{4,6},{5,7},{6,4},{7,5},{8,10},{9,11},{10,... | collective-permute-start | bytes 1572872 | tf_op jit(solution)/shard_map/ppermute | solution.py:182
  200.7 13.9 %copy-start.109 = (bf16[1024,2048]{1,0:T(8,128)(2,1)S(1)}, bf16[1024,2048]{1,0:T(8,128)(2,1)}, u32[]{:S(2)}) copy-start(bf16[1024,2048]{1,0:T(8,128)(2,1)} %all-gather.5.cloned.1.call-done) | copy-start | bytes 12582916
  200.9 13.7 %copy-start.68 = (bf16[2,2,256,1024]{3,2,1,0:T(8,128)(2,1)S(1)}, bf16[2,2,256,1024]{3,2,1,0:T(8,128)(2,1)}, u32[]{:S(2)}) copy-start(bf16[2,2,256,1024]{3,2,1,0:T(8,128)(2,1)} %copy.393) | copy-start | bytes 6291460
  200.9 13.2 %collective-permute-start.6 = (bf16[1,256,1024]{2,1,0:T(8,128)(2,1)S(1)}, bf16[1,256,1024]{2,1,0:T(8,128)(2,1)S(1)}, u32[]{:S(2)}, u32[]{:S(2)}) collective-permute-start(bf16[1,256,1024]{2,1,0:T(8,128)(2,1)S(1)} %fusion.121), channel_id=1, source_target_pairs={{0,2},{1,3},{2,0},{3,1},{4,6},{5,7},{6,4},{7,5},{8,10},{9,11},{10,... | collective-permute-start | bytes 1572872 | tf_op jit(solution)/shard_map/ppermute | solution.py:182
  214.5 2.7 collective-permute-start.7
  224.9 2.7 collective-permute-start.8
  230.2 14.3 %collective-permute-start.9 = (bf16[1,256,1024]{2,1,0:T(8,128)(2,1)}, bf16[1,256,1024]{2,1,0:T(8,128)(2,1)}, u32[]{:S(2)}, u32[]{:S(2)}) collective-permute-start(bf16[1,256,1024]{2,1,0:T(8,128)(2,1)} %dynamic-slice_convert_fusion.2), channel_id=1, source_target_pairs={{0,2},{1,3},{2,0},{3,1},{4,6},{5,7},{6,4},{7,5},{8,10},{9,11},{10,... | collective-permute-start | bytes 1572872 | tf_op jit(solution)/shard_map/ppermute | solution.py:182
  233.7 12.6 %copy-start.16 = (f32[2,256,1024]{2,1,0:T(8,128)S(1)}, f32[2,256,1024]{2,1,0:T(8,128)}, u32[]{:S(2)}) copy-start(f32[2,256,1024]{2,1,0:T(8,128)} %copy-done.15) | copy-start | bytes 6291460
  233.7 12.6 %copy-start.76 = (bf16[256,1024]{1,0:T(8,128)(2,1)S(1)}, bf16[256,1024]{1,0:T(8,128)(2,1)}, u32[]{:S(2)}) copy-start(bf16[256,1024]{1,0:T(8,128)(2,1)} %param.19) | copy-start | bytes 1572868
  248.9 13.1 %collective-permute-start.10 = (bf16[1,256,1024]{2,1,0:T(8,128)(2,1)S(1)}, bf16[1,256,1024]{2,1,0:T(8,128)(2,1)S(1)}, u32[]{:S(2)}, u32[]{:S(2)}) collective-permute-start(bf16[1,256,1024]{2,1,0:T(8,128)(2,1)S(1)} %get-tuple-element.208), channel_id=1, source_target_pairs={{0,2},{1,3},{2,0},{3,1},{4,6},{5,7},{6,4},{7,5},{8,10},{9,11},{10,... | collective-permute-start | bytes 1572872 | tf_op jit(solution)/shard_map/ppermute | solution.py:182
  252.4 9.9 %copy-start.203 = (bf16[1024,512]{0,1:T(8,128)(2,1)S(1)}, bf16[1024,512]{0,1:T(8,128)(2,1)}, u32[]{:S(2)}) copy-start(bf16[1024,512]{0,1:T(8,128)(2,1)} %get-tuple-element.228) | copy-start | bytes 3145732
  262.3 9.3 %collective-permute-start.11 = (bf16[2,256,1024]{2,1,0:T(8,128)(2,1)S(1)}, bf16[2,256,1024]{2,1,0:T(8,128)(2,1)S(1)}, u32[]{:S(2)}, u32[]{:S(2)}) collective-permute-start(bf16[2,256,1024]{2,1,0:T(8,128)(2,1)S(1)} %maximum_bitcast_fusion.3), channel_id=1, source_target_pairs={{0,1},{1,0},{2,3},{3,2},{4,5},{5,4},{6,7},{7,6},{8,9},{9,8},{10,11... | collective-permute-start | bytes 3145736 | tf_op jit(solution)/shard_map/ppermute | solution.py:182
  277.0 13.0 %copy-start.144 = (f32[384]{0:T(512)S(1)}, f32[384]{0:T(512)}, u32[]{:S(2)}) copy-start(f32[384]{0:T(512)} %mul.1141) | copy-start | bytes 4612
  329.0 79.9 %collective-permute-start.12 = (bf16[2,256,1024]{2,1,0:T(8,128)(2,1)}, bf16[2,256,1024]{2,1,0:T(8,128)(2,1)}, u32[]{:S(2)}, u32[]{:S(2)}) collective-permute-start(bf16[2,256,1024]{2,1,0:T(8,128)(2,1)} %dynamic-slice_bitcast_fusion.1), channel_id=1, source_target_pairs={{0,1},{1,0},{2,3},{3,2},{4,5},{5,4},{6,7},{7,6},{8,9},{9,8},{10,11... | collective-permute-start | bytes 3145736 | tf_op jit(solution)/shard_map/ppermute | solution.py:182
  364.6 32.8 %collective-permute-start.24 = (f32[3072]{0:T(1024)S(1)}, f32[3072]{0:T(1024)S(1)}, u32[]{:S(2)}, u32[]{:S(2)}) collective-permute-start(f32[3072]{0:T(1024)S(1)} %pad.209), channel_id=1, source_target_pairs={{0,4},{4,0},{8,12},{12,8},{16,20},{20,16},{24,28},{28,24},{1,5},{5... | collective-permute-start | bytes 36872 | tf_op jit(solution)/shard_map/ppermute | solution.py:182
  397.4 4.5 collective-permute-start.25
  401.9 5.1 collective-permute-start.26
  412.2 10.0 %copy-start.60 = (pred[512,512]{0,1:T(8,128)(4,1)S(1)}, pred[512,512]{0,1:T(8,128)(4,1)}, u32[]{:S(2)}) copy-start(pred[512,512]{0,1:T(8,128)(4,1)} %iota_compare_fusion.1) | copy-start | bytes 786436
  418.5 25.1 %collective-permute-start.13 = (bf16[1,256,1024]{2,1,0:T(8,128)(2,1)}, bf16[1,256,1024]{2,1,0:T(8,128)(2,1)}, u32[]{:S(2)}, u32[]{:S(2)}) collective-permute-start(bf16[1,256,1024]{2,1,0:T(8,128)(2,1)} %dynamic-slice_convert_fusion.1), channel_id=1, source_target_pairs={{0,2},{1,3},{2,0},{3,1},{4,6},{5,7},{6,4},{7,5},{8,10},{9,11},{10,... | collective-permute-start | bytes 1572872 | tf_op jit(solution)/shard_map/ppermute | solution.py:182
  422.0 25.3 %collective-permute-start.14 = (bf16[4,128,768]{2,1,0:T(8,128)(2,1)}, bf16[4,128,768]{2,1,0:T(8,128)(2,1)}, u32[]{:S(2)}, u32[]{:S(2)}) collective-permute-start(bf16[4,128,768]{2,1,0:T(8,128)(2,1)} %dynamic-slice_bitcast_fusion.4), channel_id=1, source_target_pairs={{0,4},{4,0},{8,12},{12,8},{16,20},{20,16},{24,28},{28,24},{1,5},{5... | collective-permute-start | bytes 2359304 | tf_op jit(solution)/shard_map/ppermute | solution.py:182
  481.3 48.6 %collective-permute-start.22 = (bf16[2,128,768]{2,1,0:T(8,128)(2,1)}, bf16[2,128,768]{2,1,0:T(8,128)(2,1)}, u32[]{:S(2)}, u32[]{:S(2)}) collective-permute-start(bf16[2,128,768]{2,1,0:T(8,128)(2,1)} %fusion.144), channel_id=1, source_target_pairs={{0,8},{4,12},{8,0},{12,4},{16,24},{20,28},{24,16},{28,20},{1,9},{5... | collective-permute-start | bytes 1179656 | tf_op jit(solution)/shard_map/ppermute | solution.py:182
  501.7 16.3 %copy-start.58 = (bf16[4,1,128,640]{3,2,0,1:T(8,128)(2,1)S(1)}, bf16[4,1,128,640]{3,2,0,1:T(8,128)(2,1)}, u32[]{:S(2)}) copy-start(bf16[4,1,128,640]{3,2,0,1:T(8,128)(2,1)} %copy.478) | copy-start | bytes 1966084
  501.7 16.3 %collective-permute-start.17 = (bf16[4,128,640]{2,1,0:T(8,128)(2,1)}, bf16[4,128,640]{2,1,0:T(8,128)(2,1)S(1)}, u32[]{:S(2)}, u32[]{:S(2)}) collective-permute-start(bf16[4,128,640]{2,1,0:T(8,128)(2,1)} %bitcast.149), channel_id=1, source_target_pairs={{0,4},{4,0},{8,12},{12,8},{16,20},{20,16},{24,28},{28,24},{1,5},{5... | collective-permute-start | bytes 1966088 | tf_op jit(solution)/shard_map/ppermute | solution.py:182
  508.6 10.9 %copy-start.67 = (bf16[128,2048]{0,1:T(8,128)(2,1)S(1)}, bf16[128,2048]{0,1:T(8,128)(2,1)}, u32[]{:S(2)}) copy-start(bf16[128,2048]{0,1:T(8,128)(2,1)} %copy.472) | copy-start | bytes 1572868
  508.6 10.9 %copy-start.26 = (bf16[1024,1024]{1,0:T(8,128)(2,1)S(1)}, bf16[1024,1024]{1,0:T(8,128)(2,1)}, u32[]{:S(2)}) copy-start(bf16[1024,1024]{1,0:T(8,128)(2,1)} %get-tuple-element.226) | copy-start | bytes 6291460
  518.9 8.4 %collective-permute-start.18 = (bf16[2,128,640]{2,1,0:T(8,128)(2,1)}, bf16[2,128,640]{2,1,0:T(8,128)(2,1)}, u32[]{:S(2)}, u32[]{:S(2)}) collective-permute-start(bf16[2,128,640]{2,1,0:T(8,128)(2,1)} %fusion.145), channel_id=1, source_target_pairs={{0,8},{4,12},{8,0},{12,4},{16,24},{20,28},{24,16},{28,20},{1,9},{5... | collective-permute-start | bytes 983048 | tf_op jit(solution)/shard_map/ppermute | solution.py:182
  520.5 9.5 %copy-start.41 = (f32[4,128,768]{2,1,0:T(8,128)S(1)}, f32[4,128,768]{2,1,0:T(8,128)}, u32[]{:S(2)}) copy-start(f32[4,128,768]{2,1,0:T(8,128)} %convert_add_fusion.4) | copy-start | bytes 4718596
  525.7 18.7 %collective-permute-start.15 = (bf16[2,256,1024]{2,1,0:T(8,128)(2,1)}, bf16[2,256,1024]{2,1,0:T(8,128)(2,1)}, u32[]{:S(2)}, u32[]{:S(2)}) collective-permute-start(bf16[2,256,1024]{2,1,0:T(8,128)(2,1)} %dynamic-slice_bitcast_fusion), channel_id=1, source_target_pairs={{0,1},{1,0},{2,3},{3,2},{4,5},{5,4},{6,7},{7,6},{8,9},{9,8},{10,11... | collective-permute-start | bytes 3145736 | tf_op jit(solution)/shard_map/ppermute | solution.py:182
  528.3 15.9 %copy-start.200 = (bf16[256]{0:T(256)(128)(2,1)S(1)}, bf16[256]{0:T(256)(128)(2,1)}, u32[]{:S(2)}) copy-start(bf16[256]{0:T(256)(128)(2,1)} %mul.1282) | copy-start | bytes 1540
  528.4 14.8 %collective-permute-start.19 = (bf16[1,128,640]{2,1,0:T(8,128)(2,1)S(1)}, bf16[1,128,640]{2,1,0:T(8,128)(2,1)S(1)}, u32[]{:S(2)}, u32[]{:S(2)}) collective-permute-start(bf16[1,128,640]{2,1,0:T(8,128)(2,1)S(1)} %dynamic-slice_convert_fusion.6), channel_id=1, source_target_pairs={{0,16},{4,20},{8,24},{12,28},{16,0},{20,4},{24,8},{28,12},{1,17},{... | collective-permute-start | bytes 491528 | tf_op jit(solution)/shard_map/ppermute | solution.py:182
  531.8 18.2 %collective-permute-start.23 = (bf16[1,128,768]{2,1,0:T(8,128)(2,1)}, bf16[1,128,768]{2,1,0:T(8,128)(2,1)}, u32[]{:S(2)}, u32[]{:S(2)}) collective-permute-start(bf16[1,128,768]{2,1,0:T(8,128)(2,1)} %dynamic-slice_convert_fusion.5), channel_id=1, source_target_pairs={{0,16},{4,20},{8,24},{12,28},{16,0},{20,4},{24,8},{28,12},{1,17},{... | collective-permute-start | bytes 589832 | tf_op jit(solution)/shard_map/ppermute | solution.py:182
  544.3 4.4 collective-permute-start.20
  547.2 21.3 %copy-start.25 = (bf16[256,1024]{1,0:T(8,128)(2,1)S(1)}, bf16[256,1024]{1,0:T(8,128)(2,1)}, u32[]{:S(2)}) copy-start(bf16[256,1024]{1,0:T(8,128)(2,1)} %param.18) | copy-start | bytes 1572868
  547.2 21.3 %copy-start.118 = (f32[1024,1]{0,1:T(1,128)S(1)}, f32[1024,1]{0,1:T(1,128)}, u32[]{:S(2)}) copy-start(f32[1024,1]{0,1:T(1,128)} %copy-done.117) | copy-start | bytes 12292
  547.2 21.3 %copy-start.172 = (f32[256]{0:T(256)S(1)}, f32[256]{0:T(256)}, u32[]{:S(2)}) copy-start(f32[256]{0:T(256)} %add_rsqrt_fusion.2) | copy-start | bytes 3076
  547.2 21.3 %collective-permute-start.16 = (bf16[1,256,1024]{2,1,0:T(8,128)(2,1)}, bf16[1,256,1024]{2,1,0:T(8,128)(2,1)}, u32[]{:S(2)}, u32[]{:S(2)}) collective-permute-start(bf16[1,256,1024]{2,1,0:T(8,128)(2,1)} %dynamic-slice_convert_fusion), channel_id=1, source_target_pairs={{0,2},{1,3},{2,0},{3,1},{4,6},{5,7},{6,4},{7,5},{8,10},{9,11},{10,... | collective-permute-start | bytes 1572872 | tf_op jit(solution)/shard_map/ppermute | solution.py:182
  549.4 15.9 %collective-permute-start.21 = (bf16[128,640]{1,0:T(8,128)(2,1)}, bf16[128,640]{1,0:T(8,128)(2,1)}, u32[]{:S(2)}, u32[]{:S(2)}) collective-permute-start(bf16[128,640]{1,0:T(8,128)(2,1)} %fusion.223), channel_id=1, source_target_pairs={{0,2},{1,3},{2,0},{3,1},{4,6},{5,7},{6,4},{7,5},{8,10},{9,11},{10,... | collective-permute-start | bytes 491528 | tf_op jit(solution)/shard_map/ppermute | solution.py:182
  (176 other events, 546.5 us)
Sparse Core Ops, SparseCore 0:
  12.0 65.7 all-gather.2
  100.1 71.5 all-gather.4
  378.5 94.9 reduce-scatter.3
